TPU v7x, 32 devices: a whole 2x2x4 slice. The times are simulated.
32 devices in a mesh: lon: 2 (over x), sec: 4 (over y, core), rad: 4 (over z).
Axes of the slice: x: 2, y: 2, z: 4, core: 2. Of those that a mesh axis runs over, the one named last changes fastest.
Arguments:
- plasma_fields: float32 [8, 64, 8, 512], P(None, 'sec', 'lon', 'rad'), may hold values from -6 to 6
- velocity: bfloat16 [3, 64, 8, 512], P(None, 'sec', 'lon', 'rad'), may hold values from -1 to 1
- resistivity: bfloat16 [64, 8, 512], P('sec', 'lon', 'rad'), may hold values from 0.0049743652 to 0.039794922
- conductance: float32 [8, 512], P('lon', 'rad'), may hold values from 0.5 to 5
- foot_map: int32 [4096, 256], P(('lon', 'sec', 'rad')), may hold values from 0 to 511
- foot_owner: int32 [4096, 1], P(('lon', 'sec', 'rad')), may hold values from 0 to 7; in each aligned block of 128 rows (0 to 127, 128 to 255, ...) at most 32 rows name the same one
- foot_row: int32 [4096], P(('lon', 'sec', 'rad')), may hold values from 0 to 31
Outputs:
- advanced_fields: float32 [8, 64, 8, 512], P(None, 'sec', 'lon', 'rad')
- potential: float32 [8, 512], P('lon', 'rad')
- foot_table: float32 [1024, 256], P(('lon', 'sec', 'rad'))
Inputs may be any that keep to these rules, and one draw needn't show every extreme that they name: `foot_owner`: in each aligned block of 128 rows (the records of one device) no owner index appears more than 32 times.
All inputs are finite; a program needn't handle non-finite values.
Results may differ from a plain program's by a relative error of at most 0.0003.
Values sent between devices are 32-bit elements; how exact they have to be, the bound alone decides.
A program may use at most 128 MiB of HBM per device.

v0:
```python
import jax
import jax.numpy as jnp
from jax import lax
from jax.sharding import PartitionSpec as P

PHASES = 4
SWEEPS = 8
ROWS_OWN = 32


COURANT = 0.25
DAMPING = 0.05
RELAX = 0.8


def with_halo(cells, sides, width, closed):
    for axis, dim in sides:
        count = lax.axis_size(axis)
        ends = count if closed else count - 1
        head = lax.slice_in_dim(cells, 0, width, axis=dim)
        tail = lax.slice_in_dim(cells, cells.shape[dim] - width, cells.shape[dim], axis=dim)
        cells = jnp.concatenate(
            [
                lax.ppermute(tail, axis, [(i, (i + 1) % count) for i in range(ends)]),
                cells,
                lax.ppermute(head, axis, [((i + 1) % count, i) for i in range(ends)]),
            ],
            axis=dim,
        )
    return cells


def broadcast(value, axis, source):
    kept = jnp.where(lax.axis_index(axis) == source, value, 0).astype(value.dtype)
    return lax.psum(kept, axis)


def advance(padded, velocity_f, resist_f):
    centre = padded[:, 1:-1, 1:-1, 1:-1]
    shell_lo = padded[:, :-2, 1:-1, 1:-1]
    shell_hi = padded[:, 2:, 1:-1, 1:-1]
    lon_lo = padded[:, 1:-1, :-2, 1:-1]
    lon_hi = padded[:, 1:-1, 2:, 1:-1]
    lat_lo = padded[:, 1:-1, 1:-1, :-2]
    lat_hi = padded[:, 1:-1, 1:-1, 2:]

    def upwind(component, lower_side, upper_side):
        return jnp.maximum(component, 0.0) * (centre - lower_side) + jnp.minimum(component, 0.0) * (
            upper_side - centre
        )

    transport = (
        upwind(velocity_f[0], shell_lo, shell_hi)
        + upwind(velocity_f[1], lon_lo, lon_hi)
        + upwind(velocity_f[2], lat_lo, lat_hi)
    )
    spread = shell_lo + shell_hi + lon_lo + lon_hi + lat_lo + lat_hi - 6.0 * centre
    return centre - COURANT * transport + resist_f * spread


def lon_faces(block):
    return with_halo(block, (("lon", 2),), 1, True)


def band_faces(block):
    return with_halo(block, (("rad", 3),), 1, False)


def relax_plane(framed, framer):
    field_lon = framed[0]
    field_lat = framed[1]
    cond_all = framed[2]
    source = (
        field_lat[2:, 1:-1] - field_lat[:-2, 1:-1] - (field_lon[1:-1, 2:] - field_lon[1:-1, :-2])
    )
    middle = cond_all[1:-1, 1:-1]
    east = 0.5 * (middle + cond_all[2:, 1:-1])
    west = 0.5 * (middle + cond_all[:-2, 1:-1])
    north = 0.5 * (middle + cond_all[1:-1, 2:])
    south = 0.5 * (middle + cond_all[1:-1, :-2])
    diagonal = DAMPING * middle + east + west + north + south
    potential = RELAX * source / diagonal
    for sweep_index in range(SWEEPS - 1):
        framed_phi = framer(potential)
        centre = framed_phi[1:-1, 1:-1]
        image = diagonal * centre - (
            east * framed_phi[2:, 1:-1]
            + west * framed_phi[:-2, 1:-1]
            + north * framed_phi[1:-1, 2:]
            + south * framed_phi[1:-1, :-2]
        )
        potential = centre + RELAX * (source - image) / diagonal
    return potential


def shards(plasma_fields, velocity, resistivity, conductance, foot_map, foot_owner, foot_row):
    velocity_f = velocity.astype(jnp.float32)
    resist_f = resistivity.astype(jnp.float32)
    current = plasma_fields
    for step_index in range(PHASES):
        padded = with_halo(lon_faces(current), (("sec", 1), ("rad", 3)), 1, False)
        current = advance(padded, velocity_f, resist_f)
    magnetic_rows = broadcast(current[5:7, 0], "sec", 0)
    base = jnp.concatenate([magnetic_rows, conductance[None]], axis=0)
    lon_count = lax.axis_size("lon")
    rad_count = lax.axis_size("rad")
    patch_lons = conductance.shape[0]
    patch_lats = conductance.shape[1]
    framed = band_faces(lon_faces(base[:, None]))[:, 0]

    def patch_framer(values):
        return band_faces(lon_faces(values[None, None]))[0, 0]

    potential = relax_plane(framed, patch_framer)
    points = foot_map.shape[1]
    record_count = foot_map.shape[0]
    owner_count = lon_count * rad_count
    capacity = 2 * record_count // owner_count
    patch_cells = patch_lons * patch_lats
    flat_patch = potential.reshape(patch_cells)
    cell_ids = jnp.arange(patch_cells, dtype=jnp.int32)

    def lookup_block(map_block):
        onehot = (map_block[:, None, :] == cell_ids[None, :, None]).astype(jnp.float32)
        return jnp.einsum(
            "c,rcp->rp",
            flat_patch,
            onehot,
            precision=lax.Precision.HIGHEST,
            preferred_element_type=jnp.float32,
        )

    records = lax.map(lookup_block, foot_map.reshape(record_count // 8, 8, points)).reshape(
        record_count, points
    )
    owners = foot_owner[:, 0]
    order_ids = jnp.arange(record_count, dtype=jnp.int32)
    before = (owners[:, None] == owners[None, :]) & (order_ids[:, None] > order_ids[None, :])
    ranks = jnp.sum(before.astype(jnp.int32), axis=1)
    slots = owners * capacity + ranks
    slot_ids = jnp.arange(owner_count * capacity, dtype=jnp.int32)
    placement = slot_ids[:, None] == slots[None, :]
    send_rows = jnp.dot(
        placement.astype(jnp.float32),
        records,
        precision=lax.Precision.HIGHEST,
        preferred_element_type=jnp.float32,
    )
    placement_int = placement.astype(jnp.int32)
    filled = jnp.sum(placement_int, axis=1)
    send_targets = jnp.dot(placement_int, foot_row) + filled - 1
    received, received_rows = (
        lax.all_to_all(
            send_rows.reshape(owner_count, capacity, points),
            ("lon", "rad"),
            split_axis=0,
            concat_axis=0,
            tiled=True,
        ),
        lax.all_to_all(
            send_targets.reshape(owner_count, capacity),
            ("lon", "rad"),
            split_axis=0,
            concat_axis=0,
            tiled=True,
        ),
    )
    received = received.reshape(-1, points)
    received_rows = received_rows.reshape(-1)
    selector = (jnp.arange(ROWS_OWN, dtype=jnp.int32)[:, None] == received_rows[None, :]).astype(
        jnp.float32
    )
    foot_table = jnp.dot(
        selector, received, precision=lax.Precision.HIGHEST, preferred_element_type=jnp.float32
    )
    return (current, potential, foot_table)


def solution(mesh):
    in_specs = (
        P(None, "sec", "lon", "rad"),
        P(None, "sec", "lon", "rad"),
        P("sec", "lon", "rad"),
        P("lon", "rad"),
        P(("lon", "sec", "rad"), None),
        P(("lon", "sec", "rad"), None),
        P(("lon", "sec", "rad")),
    )
    out_specs = (P(None, "sec", "lon", "rad"), P("lon", "rad"), P(("lon", "sec", "rad"), None))
    return jax.shard_map(shards, mesh=mesh, in_specs=in_specs, out_specs=out_specs, check_vma=False)
```

profile of v0, /device:TPU:0, one launch (start us, length us, event | category | flops | bytes accessed | tf_op | source)
XLA Modules:
  0.0 253.4 jit_solution(2682935253950836454)
XLA Ops:
  1.8 3.0 %collective-permute-start = (f32[8,16,1,128]{3,0,2,1:T(8,128)S(1)}, f32[8,16,1,128]{3,0,2,1:T(8,128)S(1)}, u32[]{:S(2)}, u32[]{:S(2)}) collective-permute-start(f32[8,16,1,128]{3,0,2,1:T(8,128)S(1)} %get-tuple-element.89), channel_id=1, source_target_pairs={{0,16},{16,0},{1,17},{17,1},{2,18},{18,2},{3,19},{19,3},{4,20},{20... | collective-permute-start | bytes 196616 | tf_op jit(solution)/shard_map/ppermute | solution.py:24
  11.8 3.5 %collective-permute-done.3 = f32[8,1,6,128]{3,0,2,1:T(8,128)S(1)} collective-permute-done((f32[8,1,6,128]{3,0,2,1:T(8,128)S(1)}, f32[8,1,6,128]{3,0,2,1:T(8,128)S(1)}, u32[]{:S(2)}, u32[]{:S(2)}) %collective-permute-start.3) | collective-permute-done | bytes 24608 | tf_op jit(solution)/shard_map/ppermute | solution.py:26
  15.9 3.6 %collective-permute-start.4 = (f32[8,18,6,1]{1,0,3,2:T(8,128)S(1)}, f32[8,18,6,1]{1,0,3,2:T(8,128)S(1)}, u32[]{:S(2)}, u32[]{:S(2)}) collective-permute-start(f32[8,18,6,1]{1,0,3,2:T(8,128)S(1)} %copy.149), channel_id=1, source_target_pairs={{0,1},{1,2},{2,3},{4,5},{5,6},{6,7},{8,9},{9,10},{10,11},{12,13},{... | collective-permute-start | bytes 10376 | tf_op jit(solution)/shard_map/ppermute | solution.py:24
  21.7 3.9 %collective-permute-done.5 = f32[8,18,6,1]{1,0,3,2:T(8,128)S(1)} collective-permute-done((f32[8,18,6,1]{1,0,3,2:T(8,128)S(1)}, f32[8,18,6,1]{1,0,3,2:T(8,128)S(1)}, u32[]{:S(2)}, u32[]{:S(2)}) %collective-permute-start.5) | collective-permute-done | bytes 3488 | tf_op jit(solution)/shard_map/ppermute | solution.py:26
  39.4 3.5 %collective-permute-start.10 = (f32[8,18,6,1]{1,0,3,2:T(8,128)S(1)}, f32[8,18,6,1]{1,0,3,2:T(8,128)S(1)}, u32[]{:S(2)}, u32[]{:S(2)}) collective-permute-start(f32[8,18,6,1]{1,0,3,2:T(8,128)S(1)} %copy.157), channel_id=1, source_target_pairs={{0,1},{1,2},{2,3},{4,5},{5,6},{6,7},{8,9},{9,10},{10,11},{12,13},{... | collective-permute-start | bytes 10376 | tf_op jit(solution)/shard_map/ppermute | solution.py:24
  45.0 4.0 %collective-permute-done.11 = f32[8,18,6,1]{1,0,3,2:T(8,128)S(1)} collective-permute-done((f32[8,18,6,1]{1,0,3,2:T(8,128)S(1)}, f32[8,18,6,1]{1,0,3,2:T(8,128)S(1)}, u32[]{:S(2)}, u32[]{:S(2)}) %collective-permute-start.11) | collective-permute-done | bytes 3488 | tf_op jit(solution)/shard_map/ppermute | solution.py:26
  62.9 3.5 %collective-permute-start.16 = (f32[8,18,6,1]{1,0,3,2:T(8,128)S(1)}, f32[8,18,6,1]{1,0,3,2:T(8,128)S(1)}, u32[]{:S(2)}, u32[]{:S(2)}) collective-permute-start(f32[8,18,6,1]{1,0,3,2:T(8,128)S(1)} %copy.161), channel_id=1, source_target_pairs={{0,1},{1,2},{2,3},{4,5},{5,6},{6,7},{8,9},{9,10},{10,11},{12,13},{... | collective-permute-start | bytes 10376 | tf_op jit(solution)/shard_map/ppermute | solution.py:24
  68.4 4.0 %collective-permute-done.17 = f32[8,18,6,1]{1,0,3,2:T(8,128)S(1)} collective-permute-done((f32[8,18,6,1]{1,0,3,2:T(8,128)S(1)}, f32[8,18,6,1]{1,0,3,2:T(8,128)S(1)}, u32[]{:S(2)}, u32[]{:S(2)}) %collective-permute-start.17) | collective-permute-done | bytes 3488 | tf_op jit(solution)/shard_map/ppermute | solution.py:26
  90.3 4.0 %collective-permute-done.23 = f32[8,18,6,1]{1,0,3,2:T(8,128)S(1)} collective-permute-done((f32[8,18,6,1]{1,0,3,2:T(8,128)S(1)}, f32[8,18,6,1]{1,0,3,2:T(8,128)S(1)}, u32[]{:S(2)}, u32[]{:S(2)}) %collective-permute-start.23) | collective-permute-done | bytes 3488 | tf_op jit(solution)/shard_map/ppermute | solution.py:26
  95.1 6.8 %psum.7 = f32[2,4,128]{2,1,0:T(4,128)S(1)} all-reduce(f32[2,4,128]{2,1,0:T(4,128)S(1)} %bitcast.81), channel_id=1, replica_groups=mesh['lon'=2,'sec'=4,'rad'=4] {'sec'}, use_global_device_ids=true, to_apply=%region_0.1 | all-reduce | flops 1024 | bytes 8192 | tf_op jit(solution)/shard_map/psum | solution.py:35
  110.3 4.2 %collective-permute-done.27 = f32[3,1,6,1]{3,2,0,1:T(8,128)S(1)} collective-permute-done((f32[3,1,6,1]{3,2,0,1:T(8,128)S(1)}, f32[3,1,6,1]{3,2,0,1:T(8,128)S(1)}, u32[]{:S(2)}, u32[]{:S(2)}) %collective-permute-start.27) | collective-permute-done | bytes 104 | tf_op jit(solution)/shard_map/ppermute | solution.py:26
  122.6 4.2 %collective-permute-done.31 = f32[1,1,6,1]{3,2,1,0:T(8,128)S(1)} collective-permute-done((f32[1,1,6,1]{3,2,1,0:T(8,128)S(1)}, f32[1,1,6,1]{3,2,1,0:T(8,128)S(1)}, u32[]{:S(2)}, u32[]{:S(2)}) %collective-permute-start.31) | collective-permute-done | bytes 56 | tf_op jit(solution)/shard_map/ppermute | solution.py:26
  135.0 4.2 %collective-permute-done.35 = f32[1,1,6,1]{3,2,1,0:T(8,128)S(1)} collective-permute-done((f32[1,1,6,1]{3,2,1,0:T(8,128)S(1)}, f32[1,1,6,1]{3,2,1,0:T(8,128)S(1)}, u32[]{:S(2)}, u32[]{:S(2)}) %collective-permute-start.35) | collective-permute-done | bytes 56 | tf_op jit(solution)/shard_map/ppermute | solution.py:26
  147.2 4.2 %collective-permute-done.39 = f32[1,1,6,1]{3,2,1,0:T(8,128)S(1)} collective-permute-done((f32[1,1,6,1]{3,2,1,0:T(8,128)S(1)}, f32[1,1,6,1]{3,2,1,0:T(8,128)S(1)}, u32[]{:S(2)}, u32[]{:S(2)}) %collective-permute-start.39) | collective-permute-done | bytes 56 | tf_op jit(solution)/shard_map/ppermute | solution.py:26
  159.6 4.2 %collective-permute-done.43 = f32[1,1,6,1]{3,2,1,0:T(8,128)S(1)} collective-permute-done((f32[1,1,6,1]{3,2,1,0:T(8,128)S(1)}, f32[1,1,6,1]{3,2,1,0:T(8,128)S(1)}, u32[]{:S(2)}, u32[]{:S(2)}) %collective-permute-start.43) | collective-permute-done | bytes 56 | tf_op jit(solution)/shard_map/ppermute | solution.py:26
  171.8 4.2 %collective-permute-done.47 = f32[1,1,6,1]{3,2,1,0:T(8,128)S(1)} collective-permute-done((f32[1,1,6,1]{3,2,1,0:T(8,128)S(1)}, f32[1,1,6,1]{3,2,1,0:T(8,128)S(1)}, u32[]{:S(2)}, u32[]{:S(2)}) %collective-permute-start.47) | collective-permute-done | bytes 56 | tf_op jit(solution)/shard_map/ppermute | solution.py:26
  179.0 3.3 %all-to-all-start = ((s32[8,1,32]{2,1,0:T(1,128)}), s32[8,1,32]{2,1,0:T(1,128)S(1)}, u32[]{:S(2)}, u32[]{:S(2)}) async-start(s32[8,1,32]{2,1,0:T(1,128)} %all_to_all.9), calls=%async_computation | async-start | bytes 8192 | tf_op jit(solution)/shard_map/all_to_all | solution.py:160
  182.4 3.8 %collective-permute-start.50 = (f32[1,1,6,1]{3,2,1,0:T(8,128)S(1)}, f32[1,1,6,1]{3,2,1,0:T(8,128)S(1)}, u32[]{:S(2)}, u32[]{:S(2)}) collective-permute-start(f32[1,1,6,1]{3,2,1,0:T(8,128)S(1)} %get-tuple-element.105), channel_id=1, source_target_pairs={{0,1},{1,2},{2,3},{4,5},{5,6},{6,7},{8,9},{9,10},{10,11},{12,13},{... | collective-permute-start | bytes 80 | tf_op jit(solution)/shard_map/ppermute | solution.py:24
  187.5 4.2 %collective-permute-done.51 = f32[1,1,6,1]{3,2,1,0:T(8,128)S(1)} collective-permute-done((f32[1,1,6,1]{3,2,1,0:T(8,128)S(1)}, f32[1,1,6,1]{3,2,1,0:T(8,128)S(1)}, u32[]{:S(2)}, u32[]{:S(2)}) %collective-permute-start.51) | collective-permute-done | bytes 56 | tf_op jit(solution)/shard_map/ppermute | solution.py:26
  197.0 3.4 %collective-permute-start.54 = (f32[1,1,6,1]{3,2,1,0:T(8,128)S(1)}, f32[1,1,6,1]{3,2,1,0:T(8,128)S(1)}, u32[]{:S(2)}, u32[]{:S(2)}) collective-permute-start(f32[1,1,6,1]{3,2,1,0:T(8,128)S(1)} %get-tuple-element.103), channel_id=1, source_target_pairs={{0,1},{1,2},{2,3},{4,5},{5,6},{6,7},{8,9},{9,10},{10,11},{12,13},{... | collective-permute-start | bytes 80 | tf_op jit(solution)/shard_map/ppermute | solution.py:24
  201.7 4.2 %collective-permute-done.55 = f32[1,1,6,1]{3,2,1,0:T(8,128)S(1)} collective-permute-done((f32[1,1,6,1]{3,2,1,0:T(8,128)S(1)}, f32[1,1,6,1]{3,2,1,0:T(8,128)S(1)}, u32[]{:S(2)}, u32[]{:S(2)}) %collective-permute-start.55) | collective-permute-done | bytes 56 | tf_op jit(solution)/shard_map/ppermute | solution.py:26
  206.1 33.5 %while.11 = (s32[]{:T(128)}, f32[16,8,256]{2,1,0:T(8,128)S(1)}, s32[16,8,256]{2,1,0:T(8,128)}, f32[512]{0:T(512)S(1)}, s32[]{:T(128)}) while((s32[]{:T(128)}, f32[16,8,256]{2,1,0:T(8,128)S(1)}, s32[16,8,256]{2,1,0:T(8,128)}, f32[512]{0:T(512)S(1)}, s32[]{:T(128)}) %tuple.72), condition=%wide.region_4.5_spmd.clone, body=%wide.region_3.4_spmd.clone.sunk | while | flops 13631490 | bytes 51269 | solution.py:133
  240.6 3.4 %all-to-all-start.1 = ((f32[8,32,256]{2,1,0:T(8,128)}), f32[8,32,256]{2,1,0:T(8,128)S(1)}, u32[]{:S(2)}, u32[]{:S(2)}) async-start(f32[8,32,256]{2,1,0:T(8,128)} %fusion.68), calls=%async_computation.1 | async-start | bytes 524288 | tf_op jit(solution)/shard_map/all_to_all | solution.py:153
  246.1 6.5 %all-to-all-done.1 = f32[8,32,256]{2,1,0:T(8,128)S(1)} async-done(((f32[8,32,256]{2,1,0:T(8,128)}), f32[8,32,256]{2,1,0:T(8,128)S(1)}, u32[]{:S(2)}, u32[]{:S(2)}) %all-to-all-start.1) | async-done | bytes 262176 | tf_op jit(solution)/shard_map/all_to_all | solution.py:153
  (259 shorter events, 158.3 us)
Async XLA Ops:
  1.8 5.4 %collective-permute-start = (f32[8,16,1,128]{3,0,2,1:T(8,128)S(1)}, f32[8,16,1,128]{3,0,2,1:T(8,128)S(1)}, u32[]{:S(2)}, u32[]{:S(2)}) collective-permute-start(f32[8,16,1,128]{3,0,2,1:T(8,128)S(1)} %get-tuple-element.89), channel_id=1, source_target_pairs={{0,16},{16,0},{1,17},{17,1},{2,18},{18,2},{3,19},{19,3},{4,20},{20... | collective-permute-start | bytes 196616 | tf_op jit(solution)/shard_map/ppermute | solution.py:24
  15.9 5.4 %collective-permute-start.4 = (f32[8,18,6,1]{1,0,3,2:T(8,128)S(1)}, f32[8,18,6,1]{1,0,3,2:T(8,128)S(1)}, u32[]{:S(2)}, u32[]{:S(2)}) collective-permute-start(f32[8,18,6,1]{1,0,3,2:T(8,128)S(1)} %copy.149), channel_id=1, source_target_pairs={{0,1},{1,2},{2,3},{4,5},{5,6},{6,7},{8,9},{9,10},{10,11},{12,13},{... | collective-permute-start | bytes 10376 | tf_op jit(solution)/shard_map/ppermute | solution.py:24
  19.9 5.7 %collective-permute-start.5 = (f32[8,18,6,1]{1,0,3,2:T(8,128)S(1)}, f32[8,18,6,1]{1,0,3,2:T(8,128)S(1)}, u32[]{:S(2)}, u32[]{:S(2)}) collective-permute-start(f32[8,18,6,1]{1,0,3,2:T(8,128)S(1)} %copy.152), channel_id=1, source_target_pairs={{1,0},{2,1},{3,2},{5,4},{6,5},{7,6},{9,8},{10,9},{11,10},{13,12},{... | collective-permute-start | bytes 10376 | tf_op jit(solution)/shard_map/ppermute | solution.py:26
  27.4 5.2 %collective-permute-start.7 = (f32[8,16,1,128]{3,0,2,1:T(8,128)S(1)}, f32[8,16,1,128]{3,0,2,1:T(8,128)S(1)}, u32[]{:S(2)}, u32[]{:S(2)}) collective-permute-start(f32[8,16,1,128]{3,0,2,1:T(8,128)S(1)} %get-tuple-element.88), channel_id=1, source_target_pairs={{16,0},{0,16},{17,1},{1,17},{18,2},{2,18},{19,3},{3,19},{20,4},{4,... | collective-permute-start | bytes 196616 | tf_op jit(solution)/shard_map/ppermute | solution.py:26
  39.4 5.2 %collective-permute-start.10 = (f32[8,18,6,1]{1,0,3,2:T(8,128)S(1)}, f32[8,18,6,1]{1,0,3,2:T(8,128)S(1)}, u32[]{:S(2)}, u32[]{:S(2)}) collective-permute-start(f32[8,18,6,1]{1,0,3,2:T(8,128)S(1)} %copy.157), channel_id=1, source_target_pairs={{0,1},{1,2},{2,3},{4,5},{5,6},{6,7},{8,9},{9,10},{10,11},{12,13},{... | collective-permute-start | bytes 10376 | tf_op jit(solution)/shard_map/ppermute | solution.py:24
  43.3 5.7 %collective-permute-start.11 = (f32[8,18,6,1]{1,0,3,2:T(8,128)S(1)}, f32[8,18,6,1]{1,0,3,2:T(8,128)S(1)}, u32[]{:S(2)}, u32[]{:S(2)}) collective-permute-start(f32[8,18,6,1]{1,0,3,2:T(8,128)S(1)} %copy.159), channel_id=1, source_target_pairs={{1,0},{2,1},{3,2},{5,4},{6,5},{7,6},{9,8},{10,9},{11,10},{13,12},{... | collective-permute-start | bytes 10376 | tf_op jit(solution)/shard_map/ppermute | solution.py:26
  50.9 5.2 %collective-permute-start.13 = (f32[8,16,1,128]{3,0,2,1:T(8,128)S(1)}, f32[8,16,1,128]{3,0,2,1:T(8,128)S(1)}, u32[]{:S(2)}, u32[]{:S(2)}) collective-permute-start(f32[8,16,1,128]{3,0,2,1:T(8,128)S(1)} %get-tuple-element.86), channel_id=1, source_target_pairs={{16,0},{0,16},{17,1},{1,17},{18,2},{2,18},{19,3},{3,19},{20,4},{4,... | collective-permute-start | bytes 196616 | tf_op jit(solution)/shard_map/ppermute | solution.py:26
  62.9 5.2 %collective-permute-start.16 = (f32[8,18,6,1]{1,0,3,2:T(8,128)S(1)}, f32[8,18,6,1]{1,0,3,2:T(8,128)S(1)}, u32[]{:S(2)}, u32[]{:S(2)}) collective-permute-start(f32[8,18,6,1]{1,0,3,2:T(8,128)S(1)} %copy.161), channel_id=1, source_target_pairs={{0,1},{1,2},{2,3},{4,5},{5,6},{6,7},{8,9},{9,10},{10,11},{12,13},{... | collective-permute-start | bytes 10376 | tf_op jit(solution)/shard_map/ppermute | solution.py:24
  66.7 5.7 %collective-permute-start.17 = (f32[8,18,6,1]{1,0,3,2:T(8,128)S(1)}, f32[8,18,6,1]{1,0,3,2:T(8,128)S(1)}, u32[]{:S(2)}, u32[]{:S(2)}) collective-permute-start(f32[8,18,6,1]{1,0,3,2:T(8,128)S(1)} %copy.163), channel_id=1, source_target_pairs={{1,0},{2,1},{3,2},{5,4},{6,5},{7,6},{9,8},{10,9},{11,10},{13,12},{... | collective-permute-start | bytes 10376 | tf_op jit(solution)/shard_map/ppermute | solution.py:26
  74.3 5.2 %collective-permute-start.19 = (f32[8,16,1,128]{3,0,2,1:T(8,128)S(1)}, f32[8,16,1,128]{3,0,2,1:T(8,128)S(1)}, u32[]{:S(2)}, u32[]{:S(2)}) collective-permute-start(f32[8,16,1,128]{3,0,2,1:T(8,128)S(1)} %get-tuple-element.84), channel_id=1, source_target_pairs={{16,0},{0,16},{17,1},{1,17},{18,2},{2,18},{19,3},{3,19},{20,4},{4,... | collective-permute-start | bytes 196616 | tf_op jit(solution)/shard_map/ppermute | solution.py:26
  88.5 5.7 %collective-permute-start.23 = (f32[8,18,6,1]{1,0,3,2:T(8,128)S(1)}, f32[8,18,6,1]{1,0,3,2:T(8,128)S(1)}, u32[]{:S(2)}, u32[]{:S(2)}) collective-permute-start(f32[8,18,6,1]{1,0,3,2:T(8,128)S(1)} %copy.167), channel_id=1, source_target_pairs={{1,0},{2,1},{3,2},{5,4},{6,5},{7,6},{9,8},{10,9},{11,10},{13,12},{... | collective-permute-start | bytes 10376 | tf_op jit(solution)/shard_map/ppermute | solution.py:26
  108.9 5.6 %collective-permute-start.27 = (f32[3,1,6,1]{3,2,0,1:T(8,128)S(1)}, f32[3,1,6,1]{3,2,0,1:T(8,128)S(1)}, u32[]{:S(2)}, u32[]{:S(2)}) collective-permute-start(f32[3,1,6,1]{3,2,0,1:T(8,128)S(1)} %get-tuple-element.100), channel_id=1, source_target_pairs={{1,0},{2,1},{3,2},{5,4},{6,5},{7,6},{9,8},{10,9},{11,10},{13,12},{... | collective-permute-start | bytes 224 | tf_op jit(solution)/shard_map/ppermute | solution.py:26
  121.3 5.5 %collective-permute-start.31 = (f32[1,1,6,1]{3,2,1,0:T(8,128)S(1)}, f32[1,1,6,1]{3,2,1,0:T(8,128)S(1)}, u32[]{:S(2)}, u32[]{:S(2)}) collective-permute-start(f32[1,1,6,1]{3,2,1,0:T(8,128)S(1)} %get-tuple-element.116), channel_id=1, source_target_pairs={{1,0},{2,1},{3,2},{5,4},{6,5},{7,6},{9,8},{10,9},{11,10},{13,12},{... | collective-permute-start | bytes 80 | tf_op jit(solution)/shard_map/ppermute | solution.py:26
  133.7 5.5 %collective-permute-start.35 = (f32[1,1,6,1]{3,2,1,0:T(8,128)S(1)}, f32[1,1,6,1]{3,2,1,0:T(8,128)S(1)}, u32[]{:S(2)}, u32[]{:S(2)}) collective-permute-start(f32[1,1,6,1]{3,2,1,0:T(8,128)S(1)} %get-tuple-element.114), channel_id=1, source_target_pairs={{1,0},{2,1},{3,2},{5,4},{6,5},{7,6},{9,8},{10,9},{11,10},{13,12},{... | collective-permute-start | bytes 80 | tf_op jit(solution)/shard_map/ppermute | solution.py:26
  145.9 5.5 %collective-permute-start.39 = (f32[1,1,6,1]{3,2,1,0:T(8,128)S(1)}, f32[1,1,6,1]{3,2,1,0:T(8,128)S(1)}, u32[]{:S(2)}, u32[]{:S(2)}) collective-permute-start(f32[1,1,6,1]{3,2,1,0:T(8,128)S(1)} %get-tuple-element.112), channel_id=1, source_target_pairs={{1,0},{2,1},{3,2},{5,4},{6,5},{7,6},{9,8},{10,9},{11,10},{13,12},{... | collective-permute-start | bytes 80 | tf_op jit(solution)/shard_map/ppermute | solution.py:26
  158.3 5.5 %collective-permute-start.43 = (f32[1,1,6,1]{3,2,1,0:T(8,128)S(1)}, f32[1,1,6,1]{3,2,1,0:T(8,128)S(1)}, u32[]{:S(2)}, u32[]{:S(2)}) collective-permute-start(f32[1,1,6,1]{3,2,1,0:T(8,128)S(1)} %get-tuple-element.110), channel_id=1, source_target_pairs={{1,0},{2,1},{3,2},{5,4},{6,5},{7,6},{9,8},{10,9},{11,10},{13,12},{... | collective-permute-start | bytes 80 | tf_op jit(solution)/shard_map/ppermute | solution.py:26
  170.5 5.5 %collective-permute-start.47 = (f32[1,1,6,1]{3,2,1,0:T(8,128)S(1)}, f32[1,1,6,1]{3,2,1,0:T(8,128)S(1)}, u32[]{:S(2)}, u32[]{:S(2)}) collective-permute-start(f32[1,1,6,1]{3,2,1,0:T(8,128)S(1)} %get-tuple-element.108), channel_id=1, source_target_pairs={{1,0},{2,1},{3,2},{5,4},{6,5},{7,6},{9,8},{10,9},{11,10},{13,12},{... | collective-permute-start | bytes 80 | tf_op jit(solution)/shard_map/ppermute | solution.py:26
  176.2 6.1 %collective-permute-start.48 = (f32[1,1,1,128]{3,2,1,0:T(1,128)S(1)}, f32[1,1,1,128]{3,2,1,0:T(1,128)S(1)}, u32[]{:S(2)}, u32[]{:S(2)}) collective-permute-start(f32[1,1,1,128]{3,2,1,0:T(1,128)S(1)} %get-tuple-element.119), channel_id=1, source_target_pairs={{0,16},{16,0},{1,17},{17,1},{2,18},{18,2},{3,19},{19,3},{4,20},{20... | collective-permute-start | bytes 1544 | tf_op jit(solution)/shard_map/ppermute | solution.py:24
  177.3 5.0 %collective-permute-start.49 = (f32[1,1,1,128]{3,2,1,0:T(1,128)S(1)}, f32[1,1,1,128]{3,2,1,0:T(1,128)S(1)}, u32[]{:S(2)}, u32[]{:S(2)}) collective-permute-start(f32[1,1,1,128]{3,2,1,0:T(1,128)S(1)} %get-tuple-element.120), channel_id=1, source_target_pairs={{16,0},{0,16},{17,1},{1,17},{18,2},{2,18},{19,3},{3,19},{20,4},{4,... | collective-permute-start | bytes 1544 | tf_op jit(solution)/shard_map/ppermute | solution.py:26
  179.0 61.6 %all-to-all-start = ((s32[8,1,32]{2,1,0:T(1,128)}), s32[8,1,32]{2,1,0:T(1,128)S(1)}, u32[]{:S(2)}, u32[]{:S(2)}) async-start(s32[8,1,32]{2,1,0:T(1,128)} %all_to_all.9), calls=%async_computation | async-start | bytes 8192 | tf_op jit(solution)/shard_map/all_to_all | solution.py:160
  182.4 5.1 %collective-permute-start.50 = (f32[1,1,6,1]{3,2,1,0:T(8,128)S(1)}, f32[1,1,6,1]{3,2,1,0:T(8,128)S(1)}, u32[]{:S(2)}, u32[]{:S(2)}) collective-permute-start(f32[1,1,6,1]{3,2,1,0:T(8,128)S(1)} %get-tuple-element.105), channel_id=1, source_target_pairs={{0,1},{1,2},{2,3},{4,5},{5,6},{6,7},{8,9},{9,10},{10,11},{12,13},{... | collective-permute-start | bytes 80 | tf_op jit(solution)/shard_map/ppermute | solution.py:24
  186.2 5.5 %collective-permute-start.51 = (f32[1,1,6,1]{3,2,1,0:T(8,128)S(1)}, f32[1,1,6,1]{3,2,1,0:T(8,128)S(1)}, u32[]{:S(2)}, u32[]{:S(2)}) collective-permute-start(f32[1,1,6,1]{3,2,1,0:T(8,128)S(1)} %get-tuple-element.106), channel_id=1, source_target_pairs={{1,0},{2,1},{3,2},{5,4},{6,5},{7,6},{9,8},{10,9},{11,10},{13,12},{... | collective-permute-start | bytes 80 | tf_op jit(solution)/shard_map/ppermute | solution.py:26
  200.4 5.5 %collective-permute-start.55 = (f32[1,1,6,1]{3,2,1,0:T(8,128)S(1)}, f32[1,1,6,1]{3,2,1,0:T(8,128)S(1)}, u32[]{:S(2)}, u32[]{:S(2)}) collective-permute-start(f32[1,1,6,1]{3,2,1,0:T(8,128)S(1)} %get-tuple-element.104), channel_id=1, source_target_pairs={{1,0},{2,1},{3,2},{5,4},{6,5},{7,6},{9,8},{10,9},{11,10},{13,12},{... | collective-permute-start | bytes 80 | tf_op jit(solution)/shard_map/ppermute | solution.py:26
  240.6 11.9 %all-to-all-start.1 = ((f32[8,32,256]{2,1,0:T(8,128)}), f32[8,32,256]{2,1,0:T(8,128)S(1)}, u32[]{:S(2)}, u32[]{:S(2)}) async-start(f32[8,32,256]{2,1,0:T(8,128)} %fusion.68), calls=%async_computation.1 | async-start | bytes 524288 | tf_op jit(solution)/shard_map/all_to_all | solution.py:153
  (41 other events, 341.3 us)
where the time goes:
time: 255 us; the launch traced here: 253 us
  waiting for transfers between devices  102 us (40%)
  starting transfers between devices  92.1 us (36%)
  matrix products  24.1 us (9%)
  local copies, waits for them, and re-layouts  22.6 us (9%)
  blocking collectives  6.79 us (3%)
  other arithmetic  4.03 us (2%)
    ppermute x28, waiting for transfers between devices, with_halo(): lax.ppermute(head, axis, [((i + 1) % count, i) for i in range(ends)])  74.8 us
    ppermute x28, starting transfers between devices, with_halo(): lax.ppermute(tail, axis, [(i, (i + 1) % count) for i in range(ends)])  54 us
    ppermute x28, starting transfers between devices, with_halo(): lax.ppermute(head, axis, [((i + 1) % count, i) for i in range(ends)])  31.4 us
    dot_general x16, matrix products, lookup_block(): jnp.einsum('c,rcp->rp', flat_patch, onehot, precision=lax.Precision.HIGHE...  22.1 us
    ppermute x28, waiting for transfers between devices, with_halo(): lax.ppermute(tail, axis, [(i, (i + 1) % count) for i in range(ends)])  21 us
    eq x16, local copies, waits for them, and re-layouts, lookup_block(): map_block[:, None, :] == cell_ids[None, :, None]  11.3 us
    psum x1, blocking collectives, broadcast(): return lax.psum(kept, axis)  6.79 us
    all_to_all x1, waiting for transfers between devices, shards(): lax.all_to_all(send_rows.reshape(owner_count, capacity, points), ('lon',...  6.48 us
  transfers between devices with their start and end apart: 58, of which 40 were waited for; matrix products, arithmetic and copies ran while one was open for 16% of the time, Pallas kernels for 0%

commit v1 on v0

v1 whole, which is shorter than its diff:
```python
import functools

import jax
import jax.numpy as jnp
from jax import lax
from jax.experimental import pallas as pl
from jax.experimental.pallas import tpu as pltpu
from jax.sharding import PartitionSpec as P

PHASES = 4
SWEEPS = 8
ROWS_OWN = 32
COURANT = 0.25
DAMPING = 0.05
RELAX = 0.8
MESH = pl.DeviceIdType.MESH
GROUPS = ((5, 7), (0, 3), (3, 5), (7, 8))


def each(count, body):
    if count <= 16:
        for i in range(count):
            body(i)
    else:
        lax.fori_loop(0, count, lambda i, c: (body(i), c)[1], 0)


def kernel(
    sizes,
    fields, vel, res, cond, fmap, fowner, frow,
    out, out_phi, out_table,
    wide, coef, cells, shell_out, shell_in, lat_out, lat_in,
    mags, conds, map_out, map_in, row_out, row_in, phis, recs, codes, select,
    halo_send, halo_recv, mag_send, mag_recv, cond_send, cond_recv, map_send, map_recv, row_send, row_recv,
):
    n_lon, n_sec, n_rad, n_fields, shells, lons, lats, cap = sizes
    me_l, me_s, me_r = lax.axis_index("lon"), lax.axis_index("sec"), lax.axis_index("rad")
    n_all, n_own = n_lon * n_sec * n_rad, n_lon * n_rad
    me_own = me_l * n_rad + me_r
    me_flat = (me_l * n_sec + me_s) * n_rad + me_r

    def place(flat):
        return (flat // (n_sec * n_rad), (flat // n_rad) % n_sec, flat % n_rad)

    def mate(owner):
        return (owner // n_rad, me_s, owner % n_rad)

    barrier = pltpu.get_barrier_semaphore()

    def greet(t, c):
        pl.semaphore_signal(barrier, inc=1, device_id=place((me_flat + t) % n_all), device_id_type=MESH)
        return c

    lax.fori_loop(1, n_all, greet, 0)

    lane = lax.broadcasted_iota(jnp.int32, (shells, lats), 1)
    lane3 = lax.broadcasted_iota(jnp.int32, (lons, shells, lats), 2)
    row3 = lax.broadcasted_iota(jnp.int32, (lons, shells, lats), 1)

    def publish(p, g, blocks):
        f0, _ = GROUPS[g]
        low = jnp.zeros((shells, lats), jnp.float32)
        high = jnp.zeros((shells, lats), jnp.float32)
        for i, block in enumerate(blocks):
            f = f0 + i
            cells[p, f, 1 : lons + 1] = block
            shell_out[p, 0, f] = block[:, 0:1, :]
            shell_out[p, 1, f] = block[:, shells - 1 : shells, :]
            for l in range(lons):
                k = i * lons + l
                low = jnp.where(lane == k, pltpu.roll(block[l], k, 1) if k else block[l], low)
                high = jnp.where(lane == k, pltpu.roll(block[l], k + 1, 1), high)
        lat_out[p, g, 0] = low
        lat_out[p, g, 1] = high

    left, right = lax.rem(me_l + n_lon - 1, n_lon), lax.rem(me_l + 1, n_lon)

    def halo(p, g, way):
        f0, f1 = GROUPS[g]
        span = pl.ds(f0, f1 - f0)
        src, dst, to = (
            (lambda: (cells.at[p, span, 1], cells.at[p, span, lons + 1], (left, me_s, me_r))),
            (lambda: (cells.at[p, span, lons], cells.at[p, span, 0], (right, me_s, me_r))),
            (lambda: (shell_out.at[p, 0, span], shell_in.at[p, 1, span], (me_l, me_s - 1, me_r))),
            (lambda: (shell_out.at[p, 1, span], shell_in.at[p, 0, span], (me_l, me_s + 1, me_r))),
            (lambda: (lat_out.at[p, g, 0], lat_in.at[p, g, 1], (me_l, me_s, me_r - 1))),
            (lambda: (lat_out.at[p, g, 1], lat_in.at[p, g, 0], (me_l, me_s, me_r + 1))),
        )[way]()
        return pltpu.make_async_remote_copy(
            src_ref=src, dst_ref=dst, send_sem=halo_send.at[p, g, way], recv_sem=halo_recv.at[p, g, way],
            device_id=to, device_id_type=MESH,
        )

    sends = (None, None, me_s > 0, me_s < n_sec - 1, me_r > 0, me_r < n_rad - 1)
    takes = (None, None, me_s < n_sec - 1, me_s > 0, me_r < n_rad - 1, me_r > 0)

    def guarded(cond_value, act):
        if cond_value is None:
            act()
        else:
            pl.when(cond_value)(act)

    def start_halo(p, g):
        for way in (0, 1, 4, 5, 2, 3):
            guarded(sends[way], lambda: halo(p, g, way).start())

    def wait_halo(p, g):
        for way in range(6):
            guarded(takes[way], lambda: halo(p, g, way).wait_recv())

    starts = []
    for g, (f0, f1) in enumerate(GROUPS):
        blocks = []
        for f in range(f0, f1):
            blocks.append(jnp.stack([fields[f, pl.ds(l, shells, stride=lons), :] for l in range(lons)]))
        publish(0, g, blocks)

    @pl.when(me_s == 0)
    def _():
        shell_in[:, 0] = jnp.zeros_like(shell_in[:, 0])

    @pl.when(me_s == n_sec - 1)
    def _():
        shell_in[:, 1] = jnp.zeros_like(shell_in[:, 1])

    @pl.when(me_r == 0)
    def _():
        lat_in[:, :, 0] = jnp.zeros_like(lat_in[:, :, 0])

    @pl.when(me_r == n_rad - 1)
    def _():
        lat_in[:, :, 1] = jnp.zeros_like(lat_in[:, :, 1])

    conds[me_own] = cond[...]

    pl.semaphore_wait(barrier, n_all - 1)

    for g in range(len(GROUPS)):
        start_halo(0, g)

    count = fmap.shape[0]
    g_row = lax.broadcasted_iota(jnp.int32, (count, count), 0)
    g_lane = lax.broadcasted_iota(jnp.int32, (count, count), 1)
    owner_c = jnp.broadcast_to(fowner[...].astype(jnp.float32), (count, count))
    row_l = jnp.broadcast_to(frow[...].astype(jnp.float32), (count, count))
    same = g_row == g_lane
    owner_l = jnp.sum(jnp.where(same, owner_c, 0.0), axis=0, keepdims=True)
    row_c = jnp.sum(jnp.where(same, row_l, 0.0), axis=1, keepdims=True)
    alike = owner_c == owner_l
    rank_l = jnp.sum(jnp.where(alike & (g_row < g_lane), 1.0, 0.0), axis=0, keepdims=True)
    rank_c = jnp.sum(jnp.where(alike & (g_row > g_lane), 1.0, 0.0), axis=1, keepdims=True)
    key_l = (owner_l * float(count) + rank_l)
    key_c = (owner_c[:, 0:1] * float(count) + rank_c)
    spot = lax.broadcasted_iota(jnp.int32, (cap, count), 0).astype(jnp.float32)
    spot_l = g_lane.astype(jnp.float32)
    ids = fmap[...]
    high_part = (ids // lats).astype(jnp.float32).astype(jnp.bfloat16)
    low_part = (ids % lats).astype(jnp.float32).astype(jnp.bfloat16)

    def gather_owner(o):
        base = jnp.asarray(o * count, jnp.int32).astype(jnp.float32)
        pick = jnp.where(spot + base == key_l, 1.0, 0.0).astype(jnp.bfloat16)
        highs = jnp.dot(pick, high_part, preferred_element_type=jnp.float32)
        lows = jnp.dot(pick, low_part, preferred_element_type=jnp.float32)
        map_out[o] = highs * float(lats) + lows
        hit = spot_l + base == key_c
        rows = jnp.sum(jnp.where(hit, row_c + 1.0, 0.0), axis=0, keepdims=True) - 1.0
        row_out[o] = jnp.broadcast_to(rows, (8, count))

    each(n_own, gather_owner)
    map_in[me_own] = map_out[me_own]
    row_in[me_own] = row_out[me_own]

    def to_mate(t, src, dst, send, recv):
        o = (me_own + t) % n_own
        return pltpu.make_async_remote_copy(
            src_ref=src(o), dst_ref=dst.at[me_own], send_sem=send.at[t], recv_sem=recv.at[t],
            device_id=mate(o), device_id_type=MESH,
        )

    def cond_copy(t):
        return to_mate(t, lambda o: conds.at[me_own], conds, cond_send, cond_recv)

    def map_copy(t):
        return to_mate(t, lambda o: map_out.at[o], map_in, map_send, map_recv)

    def row_copy(t):
        return to_mate(t, lambda o: row_out.at[o], row_in, row_send, row_recv)

    def start_mates(t, c):
        cond_copy(t).start()
        row_copy(t).start()
        map_copy(t).start()
        return c

    lax.fori_loop(1, n_own, start_mates, 0)

    wide[0:3] = vel[...].astype(jnp.float32)
    wide[3] = res[...].astype(jnp.float32)
    for l in range(lons):
        w = [wide[d, pl.ds(l, shells, stride=lons), :] for d in range(3)]
        r = wide[3, pl.ds(l, shells, stride=lons), :]
        middle = 1.0 - 6.0 * r
        for d in range(3):
            up = COURANT * jnp.maximum(w[d], 0.0)
            down = COURANT * jnp.minimum(w[d], 0.0)
            coef[1 + 2 * d, l] = r + up
            coef[2 + 2 * d, l] = r - down
            middle = middle - (up - down)
        coef[0, l] = middle

    def step(p, g, i):
        f = GROUPS[g][0] + i
        here = cells[p, f, 1 : lons + 1]
        total = coef[0] * here
        total += coef[3] * cells[p, f, 0:lons] + coef[4] * cells[p, f, 2 : lons + 2]
        lower = jnp.where(row3 == 0, shell_in[p, 0, f], pltpu.roll(here, 1, 1))
        upper = jnp.where(row3 == shells - 1, shell_in[p, 1, f], pltpu.roll(here, shells - 1, 1))
        total += coef[1] * lower + coef[2] * upper
        low_edge, high_edge = lat_in[p, g, 0], lat_in[p, g, 1]
        ks = [i * lons + l for l in range(lons)]
        low_edges = jnp.stack([pltpu.roll(low_edge, lats - k, 1) if k else low_edge for k in ks])
        high_edges = jnp.stack([pltpu.roll(high_edge, lats - 1 - k, 1) for k in ks])
        lower = jnp.where(lane3 == 0, low_edges, pltpu.roll(here, 1, 2))
        upper = jnp.where(lane3 == lats - 1, high_edges, pltpu.roll(here, lats - 1, 2))
        return total + coef[5] * lower + coef[6] * upper

    def mag_copy(t):
        return pltpu.make_async_remote_copy(
            src_ref=mags.at[me_own], dst_ref=mags.at[me_own], send_sem=mag_send.at[t],
            recv_sem=mag_recv.at[me_own], device_id=place((me_flat + t) % n_all), device_id_type=MESH,
        )

    for p in range(PHASES):
        for g, (f0, f1) in enumerate(GROUPS):
            wait_halo(p, g)
            blocks = [step(p, g, i) for i in range(f1 - f0)]
            if p < PHASES - 1:
                publish(p + 1, g, blocks)
                start_halo(p + 1, g)
                continue
            if g == 0:

                @pl.when(me_s == 0)
                def _():
                    for c in range(2):
                        for l in range(lons):
                            mags[me_own, c, l : l + 1, :] = blocks[c][l, 0:1, :]

                    def send_mag(t, c):
                        mag_copy(t).start()
                        return c

                    lax.fori_loop(1, n_all, send_mag, 0)

            for i in range(f1 - f0):
                for l in range(lons):
                    out[f0 + i, pl.ds(l, shells, stride=lons), :] = blocks[i][l]

    def wait_mates(t, c):
        cond_copy(t).wait_recv()
        row_copy(t).wait_recv()
        map_copy(t).wait_recv()
        return c

    lax.fori_loop(1, n_own, wait_mates, 0)

    def whole(get):
        return jnp.concatenate(
            [jnp.concatenate([get(i * n_rad + j) for j in range(n_rad)], axis=1) for i in range(n_lon)], axis=0
        )

    nl, nt = n_lon * lons, n_rad * lats
    t_full = lax.broadcasted_iota(jnp.int32, (nl, nt), 1)

    def lon_up(x):
        return pltpu.roll(x, nl - 1, 0)

    def lon_down(x):
        return pltpu.roll(x, 1, 0)

    def lat_up(x):
        return jnp.where(t_full == nt - 1, 0.0, pltpu.roll(x, nt - 1, 1))

    def lat_down(x):
        return jnp.where(t_full == 0, 0.0, pltpu.roll(x, 1, 1))

    c_full = whole(lambda o: conds[o])
    east = 0.5 * (c_full + lon_up(c_full))
    west = 0.5 * (c_full + lon_down(c_full))
    north = 0.5 * (c_full + lat_up(c_full))
    south = 0.5 * (c_full + lat_down(c_full))
    scale = RELAX / (DAMPING * c_full + east + west + north + south)
    east, west, north, south = east * scale, west * scale, north * scale, south * scale

    rows_at = lax.broadcasted_iota(jnp.int32, (ROWS_OWN, count), 0).astype(jnp.float32)
    per = count // cap
    for b in range(n_own // per if n_own >= per else 1):
        part = jnp.zeros((ROWS_OWN, count), jnp.float32)
        for s in range(b * per, min((b + 1) * per, n_own)):
            one = jnp.where(rows_at == row_in[s][0:1, :], 1.0, 0.0)
            off = (s * cap) % count
            part += pltpu.roll(one, off, 1) if off else one
        select[:, b * count : (b + 1) * count] = part.astype(jnp.bfloat16)
    codes[...] = map_in[...].astype(jnp.int32)

    def wait_mag(s):
        def act():
            pltpu.make_async_remote_copy(
                src_ref=mags.at[s], dst_ref=mags.at[s], send_sem=mag_send.at[0], recv_sem=mag_recv.at[s],
                device_id=(me_l, me_s, me_r), device_id_type=MESH,
            ).wait_recv()

        pl.when((me_s > 0) | (me_own != s))(act)

    each(n_own, wait_mag)

    blon = whole(lambda o: mags[o, 0])
    blat = whole(lambda o: mags[o, 1])
    source = scale * (lon_up(blat) - lon_down(blat) - (lat_up(blon) - lat_down(blon)))
    phi = source
    for _ in range(SWEEPS - 1):
        phi = (
            ((1.0 - RELAX) * phi + source)
            + (east * lon_up(phi) + west * lon_down(phi))
            + (north * lat_up(phi) + south * lat_down(phi))
        )
    for i in range(n_lon):
        for j in range(n_rad):
            phis[i * n_rad + j] = phi[i * lons : (i + 1) * lons, j * lats : (j + 1) * lats]
    out_phi[...] = phis[me_own]

    points = fmap.shape[1]

    def look_up(s):
        patch = phis[s]
        for c in range(0, points, lats):
            code = codes[s, :, c : c + lats]
            low, high = code % lats, code // lats
            value = jnp.zeros((cap, lats), jnp.float32)
            for l in range(lons):
                line = jnp.broadcast_to(patch[l : l + 1, :], (cap, lats))
                found = jnp.take_along_axis(line, low, axis=1, mode="promise_in_bounds")
                value = jnp.where(high == l, found, value)
            recs[s, :, c : c + lats] = value

    each(n_own, look_up)
    rec = recs[...].reshape(n_own * cap, points)
    first = rec.astype(jnp.bfloat16)
    rest = rec - first.astype(jnp.float32)
    second = rest.astype(jnp.bfloat16)
    third = (rest - second.astype(jnp.float32)).astype(jnp.bfloat16)
    chosen = select[...]
    out_table[...] = (
        jnp.dot(chosen, first, preferred_element_type=jnp.float32)
        + jnp.dot(chosen, second, preferred_element_type=jnp.float32)
        + jnp.dot(chosen, third, preferred_element_type=jnp.float32)
    )

    for p in range(PHASES):
        for g in range(len(GROUPS)):
            for way in range(6):
                guarded(sends[way], lambda: halo(p, g, way).wait_send())

    def sent_mates(t, c):
        cond_copy(t).wait_send()
        row_copy(t).wait_send()
        map_copy(t).wait_send()
        return c

    lax.fori_loop(1, n_own, sent_mates, 0)

    @pl.when(me_s == 0)
    def _():
        def sent_mag(t, c):
            mag_copy(t).wait_send()
            return c

        lax.fori_loop(1, n_all, sent_mag, 0)


def shards(plasma_fields, velocity, resistivity, conductance, foot_map, foot_owner, foot_row):
    n_lon, n_sec, n_rad = lax.axis_size("lon"), lax.axis_size("sec"), lax.axis_size("rad")
    n_fields, shells, lons, lats = plasma_fields.shape
    count, points = foot_map.shape
    n_own, n_all, n_groups = n_lon * n_rad, n_lon * n_sec * n_rad, len(GROUPS)
    cap = max(8, 2 * count // n_own)
    sizes = (n_lon, n_sec, n_rad, n_fields, shells, lons, lats, cap)
    f32 = jnp.float32
    dma = pltpu.SemaphoreType.DMA
    vmem = pl.BlockSpec(memory_space=pltpu.VMEM)
    current, potential, table = pl.pallas_call(
        functools.partial(kernel, sizes),
        out_shape=(
            jax.ShapeDtypeStruct((n_fields, shells * lons, lats), f32),
            jax.ShapeDtypeStruct((lons, lats), f32),
            jax.ShapeDtypeStruct((ROWS_OWN, points), f32),
        ),
        in_specs=[vmem] * 7,
        out_specs=(vmem,) * 3,
        scratch_shapes=[
            pltpu.VMEM((4, shells * lons, lats), f32),
            pltpu.VMEM((7, lons, shells, lats), f32),
            pltpu.VMEM((PHASES, n_fields, lons + 2, shells, lats), f32),
            pltpu.VMEM((PHASES, 2, n_fields, lons, 1, lats), f32),
            pltpu.VMEM((PHASES, 2, n_fields, lons, 1, lats), f32),
            pltpu.VMEM((PHASES, n_groups, 2, shells, lats), f32),
            pltpu.VMEM((PHASES, n_groups, 2, shells, lats), f32),
            pltpu.VMEM((n_own, 2, lons, lats), f32),
            pltpu.VMEM((n_own, lons, lats), f32),
            pltpu.VMEM((n_own, cap, points), f32),
            pltpu.VMEM((n_own, cap, points), f32),
            pltpu.VMEM((n_own, 8, count), f32),
            pltpu.VMEM((n_own, 8, count), f32),
            pltpu.VMEM((n_own, lons, lats), f32),
            pltpu.VMEM((n_own, cap, points), f32),
            pltpu.VMEM((n_own, cap, points), jnp.int32),
            pltpu.VMEM((ROWS_OWN, n_own * cap), jnp.bfloat16),
            dma((PHASES, n_groups, 6)),
            dma((PHASES, n_groups, 6)),
            dma((n_all,)),
            dma((n_own,)),
            dma((n_own,)),
            dma((n_own,)),
            dma((n_own,)),
            dma((n_own,)),
            dma((n_own,)),
            dma((n_own,)),
        ],
        compiler_params=pltpu.CompilerParams(
            collective_id=0, has_side_effects=True, vmem_limit_bytes=48 * 1024 * 1024
        ),
    )(
        plasma_fields.reshape(n_fields, shells * lons, lats),
        velocity.reshape(3, shells * lons, lats),
        resistivity.reshape(shells * lons, lats),
        conductance,
        foot_map,
        foot_owner,
        foot_row.reshape(1, count),
    )
    return current.reshape(plasma_fields.shape), potential, table


def solution(mesh):
    in_specs = (
        P(None, "sec", "lon", "rad"),
        P(None, "sec", "lon", "rad"),
        P("sec", "lon", "rad"),
        P("lon", "rad"),
        P(("lon", "sec", "rad"), None),
        P(("lon", "sec", "rad"), None),
        P(("lon", "sec", "rad")),
    )
    out_specs = (P(None, "sec", "lon", "rad"), P("lon", "rad"), P(("lon", "sec", "rad"), None))
    return jax.shard_map(shards, mesh=mesh, in_specs=in_specs, out_specs=out_specs, check_vma=False)
```

time: 255 us -> 37.4 us (0.15)
  waiting for transfers between devices: 102 us -> 0 us
  starting transfers between devices: 92.1 us -> 0 us
  Pallas kernels: 0 us -> 31.9 us
  matrix products: 24.1 us -> 0 us
  local copies, waits for them, and re-layouts: 22.6 us -> 4.55 us
  blocking collectives: 6.79 us -> 0 us
  other arithmetic: 4.03 us -> 0 us
    ppermute x56 -> x0, waiting for transfers between devices: 95.9 us -> none  [the longest x28 74.8 us: with_halo(): lax.ppermute(head, axis, [((i + 1) % count, i) for i in range(ends)])]
    ppermute x56 -> x0, starting transfers between devices: 85.4 us -> none  [the longest x28 54 us: with_halo(): lax.ppermute(tail, axis, [(i, (i + 1) % count) for i in range(ends)])]
    pallas_call x0 -> x1, Pallas kernels: none -> 31.9 us  [shards(): pl.pallas_call(functools.partial(kernel, sizes), out_shape=(jax.ShapeDtyp...]
    dot_general x19 -> x0, matrix products: 24.1 us -> none  [the longest x16 22.1 us: lookup_block(): jnp.einsum('c,rcp->rp', flat_patch, onehot, precision=lax.Precision.HIGHE...]
    eq x17 -> x0, local copies, waits for them, and re-layouts: 11.4 us -> none  [the longest x16 11.3 us: lookup_block(): map_block[:, None, :] == cell_ids[None, :, None]]
    psum x1 -> x0, blocking collectives: 6.79 us -> none  [broadcast(): return lax.psum(kept, axis)]
    all_to_all x2 -> x0, starting transfers between devices: 6.72 us -> none  [the longest x1 3.41 us: shards(): lax.all_to_all(send_rows.reshape(owner_count, capacity, points), ('lon',...]
    all_to_all x2 -> x0, waiting for transfers between devices: 6.48 us -> none  [the longest x1 6.48 us: shards(): lax.all_to_all(send_rows.reshape(owner_count, capacity, points), ('lon',...]
  transfers between devices with their start and end apart: 58 -> 0, of which waited for: 40 -> 0; matrix products, arithmetic and copies ran while one was open for 16% -> 0% of each run, Pallas kernels for 0% -> 0%
where the time goes in v1:
time: 37.4 us; the launch traced here: 37.2 us
  Pallas kernels  31.9 us (85%)
  local copies, waits for them, and re-layouts  4.55 us (12%)
  between operations  0.71 us (2%)
    pallas_call x1, Pallas kernels, shards(): pl.pallas_call(functools.partial(kernel, sizes), out_shape=(jax.ShapeDtyp...  31.9 us
    unnamed x16, local copies, waits for them, and re-layouts  4.55 us

profile of v1, /device:TPU:0, one launch (start us, length us, event | category | flops | bytes accessed | tf_op | source)
XLA Modules:
  0.0 37.2 jit_solution(9155723581215789263)
XLA Ops:
  0.6 0.0 copy-start.2
  0.6 0.0 copy-start.3
  0.7 0.0 copy-start.4
  0.7 0.0 copy-start.5
  0.7 0.8 %copy.10.fowner = s32[128,1]{1,0:T(8,128)S(1)} copy(s32[128,1]{0,1:T(1,128)} %param.12) | data formatting | bytes 1024 | tf_op args[5]
  1.5 0.0 copy-done.2
  1.5 0.0 copy-done.3
  1.5 0.0 copy-done.4
  1.5 0.0 copy-done.5
  1.5 0.0 copy-start
  1.5 0.9 %copy-done = f32[8,16,4,128]{3,2,1,0:T(4,128)S(1)} copy-done((f32[8,16,4,128]{3,2,1,0:T(4,128)S(1)}, f32[8,16,4,128]{3,2,1,0:T(4,128)}, u32[]{:S(2)}) %copy-start) | copy-done | bytes 262168
  2.5 0.0 copy-start.1
  2.5 0.9 %copy-done.1 = s32[128,256]{1,0:T(8,128)S(1)} copy-done((s32[128,256]{1,0:T(8,128)S(1)}, s32[128,256]{1,0:T(8,128)}, u32[]{:S(2)}) %copy-start.1) | copy-done | bytes 131096
  3.4 31.9 %shard_map.94 = (f32[8,64,128]{2,1,0:T(8,128)S(1)}, f32[4,128]{1,0:T(4,128)S(1)}, f32[32,256]{1,0:T(8,128)S(1)}) custom-call(f32[8,64,128]{2,1,0:T(8,128)S(1)} %bitcast.5, bf16[3,64,128]{2,1,0:T(8,128)(2,1)S(1)} %bitcast.7, bf16[64,128]{1,0:T(8,128)(2,1)S(1)} %bitcast.8, f32[4,128]{1,0:T(4,128)S(1)} %copy-done.4, s32[128,256]{1,0:T(8,128)S(1)} %copy-done.1, ...), custom_call_target="tpu_custom_call" | custom-call | tf_op jit(solution)/shard_map/pallas_call | solution.py:392
  35.3 0.7 %copy.14 = f32[8,16,4,128]{3,2,1,0:T(4,128)} copy(f32[8,16,4,128]{3,2,1,0:T(4,128)S(1)} %bitcast.6) | data formatting | bytes 524288
  36.0 0.6 %copy.15 = f32[4,128]{1,0:T(4,128)} copy(f32[4,128]{1,0:T(4,128)S(1)} %get-tuple-element.13) | data formatting | bytes 4096
  36.6 0.6 %copy.16 = f32[32,256]{1,0:T(8,128)} copy(f32[32,256]{1,0:T(8,128)S(1)} %get-tuple-element.14) | data formatting | bytes 65536
Async XLA Ops:
  0.6 0.8 %copy-start.2 = (bf16[3,16,4,128]{3,2,1,0:T(4,128)(2,1)S(1)}, bf16[3,16,4,128]{3,2,1,0:T(4,128)(2,1)}, u32[]{:S(2)}) copy-start(bf16[3,16,4,128]{3,2,1,0:T(4,128)(2,1)} %param.8) | copy-start | bytes 147460
  0.6 0.8 %copy-start.3 = (bf16[16,4,128]{2,1,0:T(4,128)(2,1)S(1)}, bf16[16,4,128]{2,1,0:T(4,128)(2,1)}, u32[]{:S(2)}) copy-start(bf16[16,4,128]{2,1,0:T(4,128)(2,1)} %param.9) | copy-start | bytes 49156
  0.7 0.8 %copy-start.4 = (f32[4,128]{1,0:T(4,128)S(1)}, f32[4,128]{1,0:T(4,128)}, u32[]{:S(2)}) copy-start(f32[4,128]{1,0:T(4,128)} %cond.1) | copy-start | bytes 6148
  0.7 0.8 %copy-start.5 = (s32[128]{0:T(128)S(1)}, s32[128]{0:T(128)}, u32[]{:S(2)}) copy-start(s32[128]{0:T(128)} %param.13) | copy-start | bytes 1540
  1.5 1.0 %copy-start = (f32[8,16,4,128]{3,2,1,0:T(4,128)S(1)}, f32[8,16,4,128]{3,2,1,0:T(4,128)}, u32[]{:S(2)}) copy-start(f32[8,16,4,128]{3,2,1,0:T(4,128)} %param.7) | copy-start | bytes 786436
  2.5 0.9 %copy-start.1 = (s32[128,256]{1,0:T(8,128)S(1)}, s32[128,256]{1,0:T(8,128)}, u32[]{:S(2)}) copy-start(s32[128,256]{1,0:T(8,128)} %fmap.1) | copy-start | bytes 393220

commit v2 on v1

--- a/solution.py
+++ b/solution.py
@@ -14,7 +14,8 @@
 DAMPING = 0.05
 RELAX = 0.8
 MESH = pl.DeviceIdType.MESH
-GROUPS = ((5, 7), (0, 3), (3, 5), (7, 8))
+ORDER = (5, 6, 0, 1, 2, 3, 4, 7)
+GROUPS = ((0, 2), (2, 5), (5, 8))
 
 
 def each(count, body):
@@ -27,11 +28,12 @@
 
 def kernel(
     sizes,
-    fields, vel, res, cond, fmap, fowner, frow,
-    out, out_phi, out_table,
+    fields_at, vel_at, res_at, cond_at, fmap_at, fowner_at, frow_at,
+    end_fields, end_phi, end_table,
+    out, out_phi, out_table, store_sem, fields, vel, res, cond, fmap, fowner, frow, load_sem,
     wide, coef, cells, shell_out, shell_in, lat_out, lat_in,
-    mags, conds, map_out, map_in, row_out, row_in, phis, recs, codes, select,
-    halo_send, halo_recv, mag_send, mag_recv, cond_send, cond_recv, map_send, map_recv, row_send, row_recv,
+    mags, map_out, map_in, side_out, side_in, phis, recs, codes, select,
+    halo_send, halo_recv, mag_send, mag_recv, map_send, map_recv, side_send, side_recv,
 ):
     n_lon, n_sec, n_rad, n_fields, shells, lons, lats, cap = sizes
     me_l, me_s, me_r = lax.axis_index("lon"), lax.axis_index("sec"), lax.axis_index("rad")
@@ -39,19 +41,37 @@
     me_own = me_l * n_rad + me_r
     me_flat = (me_l * n_sec + me_s) * n_rad + me_r
 
-    def place(flat):
-        return (flat // (n_sec * n_rad), (flat // n_rad) % n_sec, flat % n_rad)
-
-    def mate(owner):
-        return (owner // n_rad, me_s, owner % n_rad)
+    loads = [
+        pltpu.make_async_copy(src, dst, load_sem.at[i])
+        for i, (src, dst) in enumerate(
+            (
+                (fields_at, fields), (vel_at, vel), (res_at, res), (cond_at, cond),
+                (fmap_at, fmap), (fowner_at, fowner), (frow_at, frow),
+            )
+        )
+    ]
+    for load in loads:
+        load.start()
+
+    def turn(me, by, count):
+        return lax.rem(me + by, count)
+
+    def peer(t):
+        dl, ds, dr = t // (n_sec * n_rad), (t // n_rad) % n_sec, t % n_rad
+        return (turn(me_l, dl, n_lon), turn(me_s, ds, n_sec), turn(me_r, dr, n_rad))
+
+    def mate(t):
+        return (turn(me_l, t // n_rad, n_lon), me_s, turn(me_r, t % n_rad, n_rad))
+
+    def others(count, body):
+        if count <= 64:
+            for t in range(1, count):
+                body(t)
+        else:
+            lax.fori_loop(1, count, lambda t, c: (body(t), c)[1], 0)
 
     barrier = pltpu.get_barrier_semaphore()
-
-    def greet(t, c):
-        pl.semaphore_signal(barrier, inc=1, device_id=place((me_flat + t) % n_all), device_id_type=MESH)
-        return c
-
-    lax.fori_loop(1, n_all, greet, 0)
+    others(n_all, lambda t: pl.semaphore_signal(barrier, inc=1, device_id=peer(t), device_id_type=MESH))
 
     lane = lax.broadcasted_iota(jnp.int32, (shells, lats), 1)
     lane3 = lax.broadcasted_iota(jnp.int32, (lons, shells, lats), 2)
@@ -87,7 +107,7 @@
             (lambda: (lat_out.at[p, g, 1], lat_in.at[p, g, 0], (me_l, me_s, me_r + 1))),
         )[way]()
         return pltpu.make_async_remote_copy(
-            src_ref=src, dst_ref=dst, send_sem=halo_send.at[p, g, way], recv_sem=halo_recv.at[p, g, way],
+            src_ref=src, dst_ref=dst, send_sem=halo_send.at[way], recv_sem=halo_recv.at[p, g, way],
             device_id=to, device_id_type=MESH,
         )
 
@@ -108,10 +128,10 @@
         for way in range(6):
             guarded(takes[way], lambda: halo(p, g, way).wait_recv())
 
-    starts = []
+    loads[0].wait()
     for g, (f0, f1) in enumerate(GROUPS):
         blocks = []
-        for f in range(f0, f1):
+        for f in ORDER[f0:f1]:
             blocks.append(jnp.stack([fields[f, pl.ds(l, shells, stride=lons), :] for l in range(lons)]))
         publish(0, g, blocks)
 
@@ -131,70 +151,13 @@
     def _():
         lat_in[:, :, 1] = jnp.zeros_like(lat_in[:, :, 1])
 
-    conds[me_own] = cond[...]
-
     pl.semaphore_wait(barrier, n_all - 1)
 
     for g in range(len(GROUPS)):
         start_halo(0, g)
 
-    count = fmap.shape[0]
-    g_row = lax.broadcasted_iota(jnp.int32, (count, count), 0)
-    g_lane = lax.broadcasted_iota(jnp.int32, (count, count), 1)
-    owner_c = jnp.broadcast_to(fowner[...].astype(jnp.float32), (count, count))
-    row_l = jnp.broadcast_to(frow[...].astype(jnp.float32), (count, count))
-    same = g_row == g_lane
-    owner_l = jnp.sum(jnp.where(same, owner_c, 0.0), axis=0, keepdims=True)
-    row_c = jnp.sum(jnp.where(same, row_l, 0.0), axis=1, keepdims=True)
-    alike = owner_c == owner_l
-    rank_l = jnp.sum(jnp.where(alike & (g_row < g_lane), 1.0, 0.0), axis=0, keepdims=True)
-    rank_c = jnp.sum(jnp.where(alike & (g_row > g_lane), 1.0, 0.0), axis=1, keepdims=True)
-    key_l = (owner_l * float(count) + rank_l)
-    key_c = (owner_c[:, 0:1] * float(count) + rank_c)
-    spot = lax.broadcasted_iota(jnp.int32, (cap, count), 0).astype(jnp.float32)
-    spot_l = g_lane.astype(jnp.float32)
-    ids = fmap[...]
-    high_part = (ids // lats).astype(jnp.float32).astype(jnp.bfloat16)
-    low_part = (ids % lats).astype(jnp.float32).astype(jnp.bfloat16)
-
-    def gather_owner(o):
-        base = jnp.asarray(o * count, jnp.int32).astype(jnp.float32)
-        pick = jnp.where(spot + base == key_l, 1.0, 0.0).astype(jnp.bfloat16)
-        highs = jnp.dot(pick, high_part, preferred_element_type=jnp.float32)
-        lows = jnp.dot(pick, low_part, preferred_element_type=jnp.float32)
-        map_out[o] = highs * float(lats) + lows
-        hit = spot_l + base == key_c
-        rows = jnp.sum(jnp.where(hit, row_c + 1.0, 0.0), axis=0, keepdims=True) - 1.0
-        row_out[o] = jnp.broadcast_to(rows, (8, count))
-
-    each(n_own, gather_owner)
-    map_in[me_own] = map_out[me_own]
-    row_in[me_own] = row_out[me_own]
-
-    def to_mate(t, src, dst, send, recv):
-        o = (me_own + t) % n_own
-        return pltpu.make_async_remote_copy(
-            src_ref=src(o), dst_ref=dst.at[me_own], send_sem=send.at[t], recv_sem=recv.at[t],
-            device_id=mate(o), device_id_type=MESH,
-        )
-
-    def cond_copy(t):
-        return to_mate(t, lambda o: conds.at[me_own], conds, cond_send, cond_recv)
-
-    def map_copy(t):
-        return to_mate(t, lambda o: map_out.at[o], map_in, map_send, map_recv)
-
-    def row_copy(t):
-        return to_mate(t, lambda o: row_out.at[o], row_in, row_send, row_recv)
-
-    def start_mates(t, c):
-        cond_copy(t).start()
-        row_copy(t).start()
-        map_copy(t).start()
-        return c
-
-    lax.fori_loop(1, n_own, start_mates, 0)
-
+    loads[1].wait()
+    loads[2].wait()
     wide[0:3] = vel[...].astype(jnp.float32)
     wide[3] = res[...].astype(jnp.float32)
     for l in range(lons):
@@ -227,11 +190,66 @@
 
     def mag_copy(t):
         return pltpu.make_async_remote_copy(
-            src_ref=mags.at[me_own], dst_ref=mags.at[me_own], send_sem=mag_send.at[t],
-            recv_sem=mag_recv.at[me_own], device_id=place((me_flat + t) % n_all), device_id_type=MESH,
+            src_ref=mags.at[me_own], dst_ref=mags.at[me_own], send_sem=mag_send,
+            recv_sem=mag_recv.at[me_own], device_id=peer(t), device_id_type=MESH,
         )
 
     for p in range(PHASES):
+        if p == 1:
+            for load in loads[3:]:
+                load.wait()
+            count, points = fmap.shape
+            g_row = lax.broadcasted_iota(jnp.int32, (count, count), 0)
+            g_lane = lax.broadcasted_iota(jnp.int32, (count, count), 1)
+            owner_l = jnp.broadcast_to(fowner[...].astype(jnp.float32), (count, count))
+            row_l = jnp.broadcast_to(frow[...].astype(jnp.float32), (count, count))
+            same = g_row == g_lane
+            owner_c = jnp.sum(jnp.where(same, owner_l, 0.0), axis=1, keepdims=True)
+            row_c = jnp.sum(jnp.where(same, row_l, 0.0), axis=1, keepdims=True)
+            alike = owner_c == owner_l
+            rank_l = jnp.sum(jnp.where(alike & (g_row < g_lane), 1.0, 0.0), axis=0, keepdims=True)
+            rank_c = jnp.sum(jnp.where(alike & (g_row > g_lane), 1.0, 0.0), axis=1, keepdims=True)
+            key_l = owner_l[0:1] * float(cap) + rank_l
+            key_c = owner_c * float(count) + rank_c
+            spot = lax.broadcasted_iota(jnp.int32, (n_own * cap, count), 0).astype(jnp.float32)
+            spot_l = g_lane.astype(jnp.float32)
+            ids = fmap[...]
+            high_part = (ids // lats).astype(jnp.float32).astype(jnp.bfloat16)
+            low_part = (ids % lats).astype(jnp.float32).astype(jnp.bfloat16)
+            pick = jnp.where(spot == key_l, 1.0, 0.0).astype(jnp.bfloat16)
+            highs = jnp.dot(pick, high_part, preferred_element_type=jnp.float32)
+            lows = jnp.dot(pick, low_part, preferred_element_type=jnp.float32)
+            map_out[...] = (highs * float(lats) + lows).reshape(n_own, cap, points)
+
+            def side_owner(o):
+                base = jnp.asarray(o * count, jnp.int32).astype(jnp.float32)
+                hit = spot_l + base == key_c
+                rows = jnp.sum(jnp.where(hit, row_c + 1.0, 0.0), axis=0, keepdims=True) - 1.0
+                side_out[o, 0:8] = jnp.broadcast_to(rows, (8, count))
+                side_out[o, 8 : 8 + lons] = cond[...]
+
+            each(n_own, side_owner)
+            map_in[me_own] = map_out[me_own]
+            side_in[me_own] = side_out[me_own]
+
+            def to_mate(t, src, dst, send, recv):
+                l, _, r = mate(t)
+                return pltpu.make_async_remote_copy(
+                    src_ref=src.at[l * n_rad + r], dst_ref=dst.at[me_own], send_sem=send, recv_sem=recv.at[t],
+                    device_id=(l, me_s, r), device_id_type=MESH,
+                )
+
+            def map_copy(t):
+                return to_mate(t, map_out, map_in, map_send, map_recv)
+
+            def side_copy(t):
+                return to_mate(t, side_out, side_in, side_send, side_recv)
+
+            def start_mate(t):
+                side_copy(t).start()
+                map_copy(t).start()
+
+            others(n_own, start_mate)
         for g, (f0, f1) in enumerate(GROUPS):
             wait_halo(p, g)
             blocks = [step(p, g, i) for i in range(f1 - f0)]
@@ -247,23 +265,23 @@
                         for l in range(lons):
                             mags[me_own, c, l : l + 1, :] = blocks[c][l, 0:1, :]
 
-                    def send_mag(t, c):
-                        mag_copy(t).start()
-                        return c
-
-                    lax.fori_loop(1, n_all, send_mag, 0)
+                    others(n_all, lambda t: mag_copy(t).start())
 
             for i in range(f1 - f0):
                 for l in range(lons):
-                    out[f0 + i, pl.ds(l, shells, stride=lons), :] = blocks[i][l]
-
-    def wait_mates(t, c):
-        cond_copy(t).wait_recv()
-        row_copy(t).wait_recv()
+                    out[ORDER[f0 + i], pl.ds(l, shells, stride=lons), :] = blocks[i][l]
+
+    stores = [
+        pltpu.make_async_copy(src, dst, store_sem.at[i])
+        for i, (src, dst) in enumerate(((out, end_fields), (out_phi, end_phi), (out_table, end_table)))
+    ]
+    stores[0].start()
+
+    def wait_mate(t):
+        side_copy(t).wait_recv()
         map_copy(t).wait_recv()
-        return c
-
-    lax.fori_loop(1, n_own, wait_mates, 0)
+
+    others(n_own, wait_mate)
 
     def whole(get):
         return jnp.concatenate(
@@ -285,7 +303,7 @@
     def lat_down(x):
         return jnp.where(t_full == 0, 0.0, pltpu.roll(x, 1, 1))
 
-    c_full = whole(lambda o: conds[o])
+    c_full = whole(lambda o: side_in[o, 8 : 8 + lons])
     east = 0.5 * (c_full + lon_up(c_full))
     west = 0.5 * (c_full + lon_down(c_full))
     north = 0.5 * (c_full + lat_up(c_full))
@@ -298,7 +316,7 @@
     for b in range(n_own // per if n_own >= per else 1):
         part = jnp.zeros((ROWS_OWN, count), jnp.float32)
         for s in range(b * per, min((b + 1) * per, n_own)):
-            one = jnp.where(rows_at == row_in[s][0:1, :], 1.0, 0.0)
+            one = jnp.where(rows_at == side_in[s, 0:1, :], 1.0, 0.0)
             off = (s * cap) % count
             part += pltpu.roll(one, off, 1) if off else one
         select[:, b * count : (b + 1) * count] = part.astype(jnp.bfloat16)
@@ -307,7 +325,7 @@
     def wait_mag(s):
         def act():
             pltpu.make_async_remote_copy(
-                src_ref=mags.at[s], dst_ref=mags.at[s], send_sem=mag_send.at[0], recv_sem=mag_recv.at[s],
+                src_ref=mags.at[s], dst_ref=mags.at[s], send_sem=mag_send, recv_sem=mag_recv.at[s],
                 device_id=(me_l, me_s, me_r), device_id_type=MESH,
             ).wait_recv()
 
@@ -329,8 +347,7 @@
         for j in range(n_rad):
             phis[i * n_rad + j] = phi[i * lons : (i + 1) * lons, j * lats : (j + 1) * lats]
     out_phi[...] = phis[me_own]
-
-    points = fmap.shape[1]
+    stores[1].start()
 
     def look_up(s):
         patch = phis[s]
@@ -357,26 +374,40 @@
         + jnp.dot(chosen, third, preferred_element_type=jnp.float32)
     )
 
-    for p in range(PHASES):
-        for g in range(len(GROUPS)):
-            for way in range(6):
-                guarded(sends[way], lambda: halo(p, g, way).wait_send())
-
-    def sent_mates(t, c):
-        cond_copy(t).wait_send()
-        row_copy(t).wait_send()
-        map_copy(t).wait_send()
-        return c
-
-    lax.fori_loop(1, n_own, sent_mates, 0)
+    stores[2].start()
+
+    def sent(ref, sem):
+        pltpu.make_async_copy(ref, ref, sem).wait()
+
+    for way, ref in enumerate(
+        (
+            cells.at[:, :, 1], cells.at[:, :, lons],
+            shell_out.at[:, 0], shell_out.at[:, 1], lat_out.at[:, :, 0], lat_out.at[:, :, 1],
+        )
+    ):
+        guarded(sends[way], lambda: sent(ref, halo_send.at[way]))
+    sent(map_out.at[1:n_own], map_send)
+    sent(side_out.at[1:n_own], side_send)
 
     @pl.when(me_s == 0)
     def _():
-        def sent_mag(t, c):
-            mag_copy(t).wait_send()
-            return c
-
-        lax.fori_loop(1, n_all, sent_mag, 0)
+        for first in range(1, n_all, n_own):
+            last = min(first + n_own, n_all)
+            sent(mags.at[0 : last - first], mag_send)
+
+    for store in stores:
+        store.wait()
+
+
+def write_out(fields, phi, table, out, out_phi, out_table, sems):
+    copies = [
+        pltpu.make_async_copy(src, dst, sems.at[i])
+        for i, (src, dst) in enumerate(((fields, out), (phi, out_phi), (table, out_table)))
+    ]
+    for copy in copies:
+        copy.start()
+    for copy in copies:
+        copy.wait()
 
 
 def shards(plasma_fields, velocity, resistivity, conductance, foot_map, foot_owner, foot_row):
@@ -388,17 +419,30 @@
     sizes = (n_lon, n_sec, n_rad, n_fields, shells, lons, lats, cap)
     f32 = jnp.float32
     dma = pltpu.SemaphoreType.DMA
-    vmem = pl.BlockSpec(memory_space=pltpu.VMEM)
-    current, potential, table = pl.pallas_call(
+    hbm = pl.BlockSpec(memory_space=pltpu.HBM)
+    results = (
+        jax.ShapeDtypeStruct((n_fields, shells * lons, lats), f32),
+        jax.ShapeDtypeStruct((lons, lats), f32),
+        jax.ShapeDtypeStruct((ROWS_OWN, points), f32),
+    )
+    made = pl.pallas_call(
         functools.partial(kernel, sizes),
-        out_shape=(
-            jax.ShapeDtypeStruct((n_fields, shells * lons, lats), f32),
-            jax.ShapeDtypeStruct((lons, lats), f32),
-            jax.ShapeDtypeStruct((ROWS_OWN, points), f32),
-        ),
-        in_specs=[vmem] * 7,
-        out_specs=(vmem,) * 3,
+        out_shape=results,
+        in_specs=[hbm] * 7,
+        out_specs=(hbm,) * 3,
         scratch_shapes=[
+            pltpu.VMEM((n_fields, shells * lons, lats), f32),
+            pltpu.VMEM((lons, lats), f32),
+            pltpu.VMEM((ROWS_OWN, points), f32),
+            dma((3,)),
+            pltpu.VMEM((n_fields, shells * lons, lats), f32),
+            pltpu.VMEM((3, shells * lons, lats), velocity.dtype),
+            pltpu.VMEM((shells * lons, lats), resistivity.dtype),
+            pltpu.VMEM((lons, lats), f32),
+            pltpu.VMEM((count, points), jnp.int32),
+            pltpu.VMEM((1, count), jnp.int32),
+            pltpu.VMEM((1, count), jnp.int32),
+            dma((7,)),
             pltpu.VMEM((4, shells * lons, lats), f32),
             pltpu.VMEM((7, lons, shells, lats), f32),
             pltpu.VMEM((PHASES, n_fields, lons + 2, shells, lats), f32),
@@ -407,28 +451,25 @@
             pltpu.VMEM((PHASES, n_groups, 2, shells, lats), f32),
             pltpu.VMEM((PHASES, n_groups, 2, shells, lats), f32),
             pltpu.VMEM((n_own, 2, lons, lats), f32),
-            pltpu.VMEM((n_own, lons, lats), f32),
             pltpu.VMEM((n_own, cap, points), f32),
             pltpu.VMEM((n_own, cap, points), f32),
-            pltpu.VMEM((n_own, 8, count), f32),
-            pltpu.VMEM((n_own, 8, count), f32),
+            pltpu.VMEM((n_own, 8 + lons, count), f32),
+            pltpu.VMEM((n_own, 8 + lons, count), f32),
             pltpu.VMEM((n_own, lons, lats), f32),
             pltpu.VMEM((n_own, cap, points), f32),
             pltpu.VMEM((n_own, cap, points), jnp.int32),
             pltpu.VMEM((ROWS_OWN, n_own * cap), jnp.bfloat16),
+            dma((6,)),
             dma((PHASES, n_groups, 6)),
-            dma((PHASES, n_groups, 6)),
-            dma((n_all,)),
+            dma,
             dma((n_own,)),
+            dma,
             dma((n_own,)),
-            dma((n_own,)),
-            dma((n_own,)),
-            dma((n_own,)),
-            dma((n_own,)),
+            dma,
             dma((n_own,)),
         ],
         compiler_params=pltpu.CompilerParams(
-            collective_id=0, has_side_effects=True, vmem_limit_bytes=48 * 1024 * 1024
+            collective_id=0, has_side_effects=True, vmem_limit_bytes=64 * 1024 * 1024
         ),
     )(
         plasma_fields.reshape(n_fields, shells * lons, lats),
@@ -436,9 +477,17 @@
         resistivity.reshape(shells * lons, lats),
         conductance,
         foot_map,
-        foot_owner,
+        foot_owner.reshape(1, count),
         foot_row.reshape(1, count),
     )
+    current, potential, table = pl.pallas_call(
+        write_out,
+        out_shape=results,
+        in_specs=[hbm] * 3,
+        out_specs=(hbm,) * 3,
+        scratch_shapes=[dma((3,))],
+        compiler_params=pltpu.CompilerParams(vmem_limit_bytes=64 * 1024 * 1024),
+    )(*made)
     return current.reshape(plasma_fields.shape), potential, table
 
 

time: 37.4 us -> 42.5 us (1.14)
  Pallas kernels: 31.9 us -> 41.7 us
  local copies, waits for them, and re-layouts: 4.55 us -> 0 us
    pallas_call x1 -> x2, Pallas kernels: 31.9 us -> 41.7 us  [the longest x1 31.6 us: shards(): pl.pallas_call(functools.partial(kernel, sizes), out_shape=results, in_sp...]
    unnamed x16 -> x0, local copies, waits for them, and re-layouts: 4.55 us -> none
where the time goes in v2:
time: 42.5 us; the launch traced here: 42.4 us
  Pallas kernels  41.7 us (98%)
  between operations  0.64 us (2%)
    pallas_call x1, Pallas kernels, shards(): pl.pallas_call(functools.partial(kernel, sizes), out_shape=results, in_sp...  31.6 us
    pallas_call x1, Pallas kernels, shards(): pl.pallas_call(write_out, out_shape=results, in_specs=[hbm] * 3, out_spec...  10.1 us

profile of v2, /device:TPU:0, one launch (start us, length us, event | category | flops | bytes accessed | tf_op | source)
XLA Modules:
  0.0 42.4 jit_solution(13434255294936984028)
XLA Ops:
  0.6 31.6 %shard_map.94 = (f32[8,64,128]{2,1,0:T(8,128)}, f32[4,128]{1,0:T(4,128)}, f32[32,256]{1,0:T(8,128)}) custom-call(f32[8,64,128]{2,1,0:T(8,128)} %bitcast.6, bf16[3,64,128]{2,1,0:T(8,128)(2,1)} %bitcast.7, bf16[64,128]{1,0:T(8,128)(2,1)} %bitcast.8, f32[4,128]{1,0:T(4,128)} %cond_at.1, s32[128,256]{1,0:T(8,128)} %fmap_at.1, s32[1,128]{1,0:T(1,128)} %bitcast.9, ...), custom_call_target="tpu_custom_call" | custom-call | tf_op jit(solution)/shard_map/pallas_call | solution.py:428
  32.3 10.1 %shard_map.95 = (f32[8,64,128]{2,1,0:T(8,128)}, f32[4,128]{1,0:T(4,128)}, f32[32,256]{1,0:T(8,128)}) custom-call(f32[8,64,128]{2,1,0:T(8,128)} %get-tuple-element.9.fields, f32[4,128]{1,0:T(4,128)} %get-tuple-element.10.phi, f32[32,256]{1,0:T(8,128)} %get-tuple-element.11.table), custom_call_target="tpu_custom_call" | custom-call | tf_op jit(solution)/shard_map/pallas_call | solution.py:483

commit v3 on v2

--- a/solution.py
+++ b/solution.py
@@ -121,7 +121,7 @@
             pl.when(cond_value)(act)
 
     def start_halo(p, g):
-        for way in (0, 1, 4, 5, 2, 3):
+        for way in (4, 5, 2, 3, 0, 1):
             guarded(sends[way], lambda: halo(p, g, way).start())
 
     def wait_halo(p, g):
@@ -155,6 +155,62 @@
 
     for g in range(len(GROUPS)):
         start_halo(0, g)
+
+    for load in loads[3:]:
+        load.wait()
+    count, points = fmap.shape
+    g_row = lax.broadcasted_iota(jnp.int32, (count, count), 0)
+    g_lane = lax.broadcasted_iota(jnp.int32, (count, count), 1)
+    owner_l = jnp.broadcast_to(fowner[...].astype(jnp.float32), (count, count))
+    row_l = jnp.broadcast_to(frow[...].astype(jnp.float32), (count, count))
+    same = g_row == g_lane
+    owner_c = jnp.sum(jnp.where(same, owner_l, 0.0), axis=1, keepdims=True)
+    row_c = jnp.sum(jnp.where(same, row_l, 0.0), axis=1, keepdims=True)
+    alike = owner_c == owner_l
+    rank_l = jnp.sum(jnp.where(alike & (g_row < g_lane), 1.0, 0.0), axis=0, keepdims=True)
+    rank_c = jnp.sum(jnp.where(alike & (g_row > g_lane), 1.0, 0.0), axis=1, keepdims=True)
+    key_l = owner_l[0:1] * float(cap) + rank_l
+    key_c = owner_c * float(count) + rank_c
+    spot = lax.broadcasted_iota(jnp.int32, (n_own * cap, count), 0).astype(jnp.float32)
+    spot_l = g_lane.astype(jnp.float32)
+    ids = fmap[...]
+    high_part = (ids // lats).astype(jnp.float32).astype(jnp.bfloat16)
+    low_part = (ids % lats).astype(jnp.float32).astype(jnp.bfloat16)
+    pick = jnp.where(spot == key_l, 1.0, 0.0).astype(jnp.bfloat16)
+    highs = jnp.dot(pick, high_part, preferred_element_type=jnp.float32)
+    lows = jnp.dot(pick, low_part, preferred_element_type=jnp.float32)
+    map_out[...] = (highs * float(lats) + lows).reshape(n_own, cap, points)
+
+    def side_owner(o):
+        base = jnp.asarray(o * count, jnp.int32).astype(jnp.float32)
+        hit = spot_l + base == key_c
+        rows = jnp.sum(jnp.where(hit, row_c + 1.0, 0.0), axis=0, keepdims=True) - 1.0
+        side_out[o, 0:8] = jnp.broadcast_to(rows, (8, count))
+        side_out[o, 8 : 8 + lons] = cond[...]
+
+    each(n_own, side_owner)
+    map_in[me_own] = map_out[me_own]
+    side_in[me_own] = side_out[me_own]
+
+    def to_mate(t, src, dst, send, recv):
+        l, _, r = mate(t)
+        return pltpu.make_async_remote_copy(
+            src_ref=src.at[l * n_rad + r], dst_ref=dst.at[me_own], send_sem=send, recv_sem=recv.at[t],
+            device_id=(l, me_s, r), device_id_type=MESH,
+        )
+
+    def map_copy(t):
+        return to_mate(t, map_out, map_in, map_send, map_recv)
+
+    def side_copy(t):
+        return to_mate(t, side_out, side_in, side_send, side_recv)
+
+    def start_mate(t):
+        side_copy(t).start()
+        map_copy(t).start()
+
+    if n_own > 64:
+        others(n_own, start_mate)
 
     loads[1].wait()
     loads[2].wait()
@@ -195,61 +251,8 @@
         )
 
     for p in range(PHASES):
-        if p == 1:
-            for load in loads[3:]:
-                load.wait()
-            count, points = fmap.shape
-            g_row = lax.broadcasted_iota(jnp.int32, (count, count), 0)
-            g_lane = lax.broadcasted_iota(jnp.int32, (count, count), 1)
-            owner_l = jnp.broadcast_to(fowner[...].astype(jnp.float32), (count, count))
-            row_l = jnp.broadcast_to(frow[...].astype(jnp.float32), (count, count))
-            same = g_row == g_lane
-            owner_c = jnp.sum(jnp.where(same, owner_l, 0.0), axis=1, keepdims=True)
-            row_c = jnp.sum(jnp.where(same, row_l, 0.0), axis=1, keepdims=True)
-            alike = owner_c == owner_l
-            rank_l = jnp.sum(jnp.where(alike & (g_row < g_lane), 1.0, 0.0), axis=0, keepdims=True)
-            rank_c = jnp.sum(jnp.where(alike & (g_row > g_lane), 1.0, 0.0), axis=1, keepdims=True)
-            key_l = owner_l[0:1] * float(cap) + rank_l
-            key_c = owner_c * float(count) + rank_c
-            spot = lax.broadcasted_iota(jnp.int32, (n_own * cap, count), 0).astype(jnp.float32)
-            spot_l = g_lane.astype(jnp.float32)
-            ids = fmap[...]
-            high_part = (ids // lats).astype(jnp.float32).astype(jnp.bfloat16)
-            low_part = (ids % lats).astype(jnp.float32).astype(jnp.bfloat16)
-            pick = jnp.where(spot == key_l, 1.0, 0.0).astype(jnp.bfloat16)
-            highs = jnp.dot(pick, high_part, preferred_element_type=jnp.float32)
-            lows = jnp.dot(pick, low_part, preferred_element_type=jnp.float32)
-            map_out[...] = (highs * float(lats) + lows).reshape(n_own, cap, points)
-
-            def side_owner(o):
-                base = jnp.asarray(o * count, jnp.int32).astype(jnp.float32)
-                hit = spot_l + base == key_c
-                rows = jnp.sum(jnp.where(hit, row_c + 1.0, 0.0), axis=0, keepdims=True) - 1.0
-                side_out[o, 0:8] = jnp.broadcast_to(rows, (8, count))
-                side_out[o, 8 : 8 + lons] = cond[...]
-
-            each(n_own, side_owner)
-            map_in[me_own] = map_out[me_own]
-            side_in[me_own] = side_out[me_own]
-
-            def to_mate(t, src, dst, send, recv):
-                l, _, r = mate(t)
-                return pltpu.make_async_remote_copy(
-                    src_ref=src.at[l * n_rad + r], dst_ref=dst.at[me_own], send_sem=send, recv_sem=recv.at[t],
-                    device_id=(l, me_s, r), device_id_type=MESH,
-                )
-
-            def map_copy(t):
-                return to_mate(t, map_out, map_in, map_send, map_recv)
-
-            def side_copy(t):
-                return to_mate(t, side_out, side_in, side_send, side_recv)
-
-            def start_mate(t):
-                side_copy(t).start()
-                map_copy(t).start()
-
-            others(n_own, start_mate)
+        for t in range(1 + p, n_own, PHASES) if n_own <= 64 else ():
+            start_mate(t)
         for g, (f0, f1) in enumerate(GROUPS):
             wait_halo(p, g)
             blocks = [step(p, g, i) for i in range(f1 - f0)]
@@ -399,15 +402,21 @@
         store.wait()
 
 
-def write_out(fields, phi, table, out, out_phi, out_table, sems):
-    copies = [
-        pltpu.make_async_copy(src, dst, sems.at[i])
-        for i, (src, dst) in enumerate(((fields, out), (phi, out_phi), (table, out_table)))
-    ]
-    for copy in copies:
-        copy.start()
-    for copy in copies:
-        copy.wait()
+def write_out(fields, phi, table, out, out_phi, out_table, held, held_phi, held_table, sems):
+    pieces = [(phi, held_phi, out_phi), (table, held_table, out_table)]
+    count = fields.shape[0]
+    for f in range(0, count, 2):
+        span = pl.ds(f, 2)
+        pieces.insert(len(pieces) - 2, (fields.at[span], held.at[span], out.at[span]))
+    loads = [pltpu.make_async_copy(a, b, sems.at[0, i]) for i, (a, b, _) in enumerate(pieces)]
+    stores = [pltpu.make_async_copy(b, c, sems.at[1, i]) for i, (_, b, c) in enumerate(pieces)]
+    for load in loads:
+        load.start()
+    for load, store in zip(loads, stores):
+        load.wait()
+        store.start()
+    for store in stores:
+        store.wait()
 
 
 def shards(plasma_fields, velocity, resistivity, conductance, foot_map, foot_owner, foot_row):
@@ -485,7 +494,7 @@
         out_shape=results,
         in_specs=[hbm] * 3,
         out_specs=(hbm,) * 3,
-        scratch_shapes=[dma((3,))],
+        scratch_shapes=[pltpu.VMEM(r.shape, r.dtype) for r in results] + [dma((2, 2 + n_fields // 2))],
         compiler_params=pltpu.CompilerParams(vmem_limit_bytes=64 * 1024 * 1024),
     )(*made)
     return current.reshape(plasma_fields.shape), potential, table

time: 42.5 us -> 31.6 us (0.74)
  Pallas kernels: 41.7 us -> 30.8 us
    pallas_call x1, Pallas kernels: 10.1 us -> 1.68 us  [shards(): pl.pallas_call(write_out, out_shape=results, in_specs=[hbm] * 3, out_spec...]
    pallas_call x1, Pallas kernels: 31.6 us -> 29.1 us  [shards(): pl.pallas_call(functools.partial(kernel, sizes), out_shape=results, in_sp...]
where the time goes in v3:
time: 31.6 us; the launch traced here: 31.4 us
  Pallas kernels  30.8 us (97%)
  between operations  0.64 us (2%)
    pallas_call x1, Pallas kernels, shards(): pl.pallas_call(functools.partial(kernel, sizes), out_shape=results, in_sp...  29.1 us
    pallas_call x1, Pallas kernels, shards(): pl.pallas_call(write_out, out_shape=results, in_specs=[hbm] * 3, out_spec...  1.68 us

profile of v3, /device:TPU:0, one launch (start us, length us, event | category | flops | bytes accessed | tf_op | source)
XLA Modules:
  0.0 31.4 jit_solution(4195943860754144326)
XLA Ops:
  0.6 29.1 %shard_map.94 = (f32[8,64,128]{2,1,0:T(8,128)}, f32[4,128]{1,0:T(4,128)}, f32[32,256]{1,0:T(8,128)}) custom-call(f32[8,64,128]{2,1,0:T(8,128)} %bitcast.6, bf16[3,64,128]{2,1,0:T(8,128)(2,1)} %bitcast.7, bf16[64,128]{1,0:T(8,128)(2,1)} %bitcast.8, f32[4,128]{1,0:T(4,128)} %cond_at.1, s32[128,256]{1,0:T(8,128)} %fmap_at.1, s32[1,128]{1,0:T(1,128)} %bitcast.9, ...), custom_call_target="tpu_custom_call" | custom-call | tf_op jit(solution)/shard_map/pallas_call | solution.py:437
  29.7 1.7 %shard_map.95 = (f32[8,64,128]{2,1,0:T(8,128)}, f32[4,128]{1,0:T(4,128)}, f32[32,256]{1,0:T(8,128)}) custom-call(f32[8,64,128]{2,1,0:T(8,128)} %get-tuple-element.9.fields, f32[4,128]{1,0:T(4,128)} %get-tuple-element.10.phi, f32[32,256]{1,0:T(8,128)} %get-tuple-element.11.table), custom_call_target="tpu_custom_call" | custom-call | tf_op jit(solution)/shard_map/pallas_call | solution.py:492

commit v4 on v3

--- a/solution.py
+++ b/solution.py
@@ -250,35 +250,44 @@
             recv_sem=mag_recv.at[me_own], device_id=peer(t), device_id_type=MESH,
         )
 
-    for p in range(PHASES):
-        for t in range(1 + p, n_own, PHASES) if n_own <= 64 else ():
+    stores = []
+
+    def store(src, dst):
+        copy = pltpu.make_async_copy(src, dst, store_sem.at[len(stores)])
+        copy.start()
+        stores.append(copy)
+
+    def run(p, g):
+        f0, f1 = GROUPS[g]
+        wait_halo(p, g)
+        blocks = [step(p, g, i) for i in range(f1 - f0)]
+        if p < PHASES - 1:
+            publish(p + 1, g, blocks)
+            start_halo(p + 1, g)
+            return
+        if g == 0:
+
+            @pl.when(me_s == 0)
+            def _():
+                for c in range(2):
+                    for l in range(lons):
+                        mags[me_own, c, l : l + 1, :] = blocks[c][l, 0:1, :]
+                others(n_all, lambda t: mag_copy(t).start())
+
+        for i in range(f1 - f0):
+            for l in range(lons):
+                out[ORDER[f0 + i], pl.ds(l, shells, stride=lons), :] = blocks[i][l]
+        for f in ORDER[f0:f1]:
+            store(out.at[f], end_fields.at[f])
+
+    for p in range(PHASES - 1):
+        for t in range(1 + p, n_own, PHASES - 1) if n_own <= 64 else ():
             start_mate(t)
-        for g, (f0, f1) in enumerate(GROUPS):
-            wait_halo(p, g)
-            blocks = [step(p, g, i) for i in range(f1 - f0)]
-            if p < PHASES - 1:
-                publish(p + 1, g, blocks)
-                start_halo(p + 1, g)
-                continue
-            if g == 0:
-
-                @pl.when(me_s == 0)
-                def _():
-                    for c in range(2):
-                        for l in range(lons):
-                            mags[me_own, c, l : l + 1, :] = blocks[c][l, 0:1, :]
-
-                    others(n_all, lambda t: mag_copy(t).start())
-
-            for i in range(f1 - f0):
-                for l in range(lons):
-                    out[ORDER[f0 + i], pl.ds(l, shells, stride=lons), :] = blocks[i][l]
-
-    stores = [
-        pltpu.make_async_copy(src, dst, store_sem.at[i])
-        for i, (src, dst) in enumerate(((out, end_fields), (out_phi, end_phi), (out_table, end_table)))
-    ]
-    stores[0].start()
+        run(p, 0)
+        run(p, 1)
+        if p == PHASES - 2:
+            run(p + 1, 0)
+        run(p, 2)
 
     def wait_mate(t):
         side_copy(t).wait_recv()
@@ -350,7 +359,7 @@
         for j in range(n_rad):
             phis[i * n_rad + j] = phi[i * lons : (i + 1) * lons, j * lats : (j + 1) * lats]
     out_phi[...] = phis[me_own]
-    stores[1].start()
+    store(out_phi, end_phi)
 
     def look_up(s):
         patch = phis[s]
@@ -377,7 +386,10 @@
         + jnp.dot(chosen, third, preferred_element_type=jnp.float32)
     )
 
-    stores[2].start()
+    store(out_table, end_table)
+
+    run(PHASES - 1, 1)
+    run(PHASES - 1, 2)
 
     def sent(ref, sem):
         pltpu.make_async_copy(ref, ref, sem).wait()
@@ -398,8 +410,8 @@
             last = min(first + n_own, n_all)
             sent(mags.at[0 : last - first], mag_send)
 
-    for store in stores:
-        store.wait()
+    for copy in stores:
+        copy.wait()
 
 
 def write_out(fields, phi, table, out, out_phi, out_table, held, held_phi, held_table, sems):
@@ -415,8 +427,8 @@
     for load, store in zip(loads, stores):
         load.wait()
         store.start()
-    for store in stores:
-        store.wait()
+    for copy in stores:
+        copy.wait()
 
 
 def shards(plasma_fields, velocity, resistivity, conductance, foot_map, foot_owner, foot_row):
@@ -443,7 +455,7 @@
             pltpu.VMEM((n_fields, shells * lons, lats), f32),
             pltpu.VMEM((lons, lats), f32),
             pltpu.VMEM((ROWS_OWN, points), f32),
-            dma((3,)),
+            dma((2 + n_fields,)),
             pltpu.VMEM((n_fields, shells * lons, lats), f32),
             pltpu.VMEM((3, shells * lons, lats), velocity.dtype),
             pltpu.VMEM((shells * lons, lats), resistivity.dtype),

time: 31.6 us -> 32.2 us (1.019)
  Pallas kernels: 30.8 us -> 31.4 us
    pallas_call x1, Pallas kernels: 29.1 us -> 29.7 us  [shards(): pl.pallas_call(functools.partial(kernel, sizes), out_shape=results, in_sp...]
where the time goes in v4:
time: 32.2 us; the launch traced here: 32 us
  Pallas kernels  31.4 us (98%)
  between operations  0.64 us (2%)
    pallas_call x1, Pallas kernels, shards(): pl.pallas_call(functools.partial(kernel, sizes), out_shape=results, in_sp...  29.7 us
    pallas_call x1, Pallas kernels, shards(): pl.pallas_call(write_out, out_shape=results, in_specs=[hbm] * 3, out_spec...  1.68 us

profile of v4, /device:TPU:0, one launch (start us, length us, event | category | flops | bytes accessed | tf_op | source)
XLA Modules:
  0.0 32.0 jit_solution(15439760031680163081)
XLA Ops:
  0.6 29.7 %shard_map.94 = (f32[8,64,128]{2,1,0:T(8,128)}, f32[4,128]{1,0:T(4,128)}, f32[32,256]{1,0:T(8,128)}) custom-call(f32[8,64,128]{2,1,0:T(8,128)} %bitcast.6, bf16[3,64,128]{2,1,0:T(8,128)(2,1)} %bitcast.7, bf16[64,128]{1,0:T(8,128)(2,1)} %bitcast.8, f32[4,128]{1,0:T(4,128)} %cond_at.1, s32[128,256]{1,0:T(8,128)} %fmap_at.1, s32[1,128]{1,0:T(1,128)} %bitcast.9, ...), custom_call_target="tpu_custom_call" | custom-call | tf_op jit(solution)/shard_map/pallas_call | solution.py:449
  30.3 1.7 %shard_map.95 = (f32[8,64,128]{2,1,0:T(8,128)}, f32[4,128]{1,0:T(4,128)}, f32[32,256]{1,0:T(8,128)}) custom-call(f32[8,64,128]{2,1,0:T(8,128)} %get-tuple-element.9.fields, f32[4,128]{1,0:T(4,128)} %get-tuple-element.10.phi, f32[32,256]{1,0:T(8,128)} %get-tuple-element.11.table), custom_call_target="tpu_custom_call" | custom-call | tf_op jit(solution)/shard_map/pallas_call | solution.py:504

commit v5 on v4

--- a/solution.py
+++ b/solution.py
@@ -15,7 +15,7 @@
 RELAX = 0.8
 MESH = pl.DeviceIdType.MESH
 ORDER = (5, 6, 0, 1, 2, 3, 4, 7)
-GROUPS = ((0, 2), (2, 5), (5, 8))
+GROUPS = ((0, 2), (2, 8))
 
 
 def each(count, body):
@@ -32,14 +32,13 @@
     end_fields, end_phi, end_table,
     out, out_phi, out_table, store_sem, fields, vel, res, cond, fmap, fowner, frow, load_sem,
     wide, coef, cells, shell_out, shell_in, lat_out, lat_in,
-    mags, map_out, map_in, side_out, side_in, phis, recs, codes, select,
-    halo_send, halo_recv, mag_send, mag_recv, map_send, map_recv, side_send, side_recv,
+    mags, map_out, map_in, phis, recs, codes, select,
+    halo_send, halo_recv, mag_send, mag_recv, map_send, map_recv,
 ):
     n_lon, n_sec, n_rad, n_fields, shells, lons, lats, cap = sizes
     me_l, me_s, me_r = lax.axis_index("lon"), lax.axis_index("sec"), lax.axis_index("rad")
-    n_all, n_own = n_lon * n_sec * n_rad, n_lon * n_rad
+    n_own = n_lon * n_rad
     me_own = me_l * n_rad + me_r
-    me_flat = (me_l * n_sec + me_s) * n_rad + me_r
 
     loads = [
         pltpu.make_async_copy(src, dst, load_sem.at[i])
@@ -56,9 +55,8 @@
     def turn(me, by, count):
         return lax.rem(me + by, count)
 
-    def peer(t):
-        dl, ds, dr = t // (n_sec * n_rad), (t // n_rad) % n_sec, t % n_rad
-        return (turn(me_l, dl, n_lon), turn(me_s, ds, n_sec), turn(me_r, dr, n_rad))
+    def above(t):
+        return (me_l, turn(me_s, t, n_sec), me_r)
 
     def mate(t):
         return (turn(me_l, t // n_rad, n_lon), me_s, turn(me_r, t % n_rad, n_rad))
@@ -71,7 +69,8 @@
             lax.fori_loop(1, count, lambda t, c: (body(t), c)[1], 0)
 
     barrier = pltpu.get_barrier_semaphore()
-    others(n_all, lambda t: pl.semaphore_signal(barrier, inc=1, device_id=peer(t), device_id_type=MESH))
+    others(n_sec, lambda t: pl.semaphore_signal(barrier, inc=1, device_id=above(t), device_id_type=MESH))
+    others(n_own, lambda t: pl.semaphore_signal(barrier, inc=1, device_id=mate(t), device_id_type=MESH))
 
     lane = lax.broadcasted_iota(jnp.int32, (shells, lats), 1)
     lane3 = lax.broadcasted_iota(jnp.int32, (lons, shells, lats), 2)
@@ -151,7 +150,7 @@
     def _():
         lat_in[:, :, 1] = jnp.zeros_like(lat_in[:, :, 1])
 
-    pl.semaphore_wait(barrier, n_all - 1)
+    pl.semaphore_wait(barrier, n_sec - 1 + n_own - 1)
 
     for g in range(len(GROUPS)):
         start_halo(0, g)
@@ -179,18 +178,17 @@
     pick = jnp.where(spot == key_l, 1.0, 0.0).astype(jnp.bfloat16)
     highs = jnp.dot(pick, high_part, preferred_element_type=jnp.float32)
     lows = jnp.dot(pick, low_part, preferred_element_type=jnp.float32)
-    map_out[...] = (highs * float(lats) + lows).reshape(n_own, cap, points)
+    map_out[:, 0:cap, :] = (highs * float(lats) + lows).reshape(n_own, cap, points)
 
     def side_owner(o):
         base = jnp.asarray(o * count, jnp.int32).astype(jnp.float32)
         hit = spot_l + base == key_c
         rows = jnp.sum(jnp.where(hit, row_c + 1.0, 0.0), axis=0, keepdims=True) - 1.0
-        side_out[o, 0:8] = jnp.broadcast_to(rows, (8, count))
-        side_out[o, 8 : 8 + lons] = cond[...]
+        map_out[o, cap : cap + 8, 0:count] = jnp.broadcast_to(rows, (8, count))
+        map_out[o, cap : cap + lons, count : count + lats] = cond[...]
 
     each(n_own, side_owner)
     map_in[me_own] = map_out[me_own]
-    side_in[me_own] = side_out[me_own]
 
     def to_mate(t, src, dst, send, recv):
         l, _, r = mate(t)
@@ -202,11 +200,7 @@
     def map_copy(t):
         return to_mate(t, map_out, map_in, map_send, map_recv)
 
-    def side_copy(t):
-        return to_mate(t, side_out, side_in, side_send, side_recv)
-
     def start_mate(t):
-        side_copy(t).start()
         map_copy(t).start()
 
     if n_own > 64:
@@ -244,10 +238,10 @@
         upper = jnp.where(lane3 == lats - 1, high_edges, pltpu.roll(here, lats - 1, 2))
         return total + coef[5] * lower + coef[6] * upper
 
-    def mag_copy(t):
+    def mag_copy(to, sem):
         return pltpu.make_async_remote_copy(
-            src_ref=mags.at[me_own], dst_ref=mags.at[me_own], send_sem=mag_send,
-            recv_sem=mag_recv.at[me_own], device_id=peer(t), device_id_type=MESH,
+            src_ref=mags.at[me_own], dst_ref=mags.at[me_own], send_sem=mag_send.at[sem],
+            recv_sem=mag_recv.at[me_own], device_id=to, device_id_type=MESH,
         )
 
     stores = []
@@ -272,7 +266,8 @@
                 for c in range(2):
                     for l in range(lons):
                         mags[me_own, c, l : l + 1, :] = blocks[c][l, 0:1, :]
-                others(n_all, lambda t: mag_copy(t).start())
+                others(n_sec, lambda t: mag_copy(above(t), 0).start())
+                others(n_own, lambda t: mag_copy(mate(t), 1).start())
 
         for i in range(f1 - f0):
             for l in range(lons):
@@ -283,17 +278,11 @@
     for p in range(PHASES - 1):
         for t in range(1 + p, n_own, PHASES - 1) if n_own <= 64 else ():
             start_mate(t)
-        run(p, 0)
-        run(p, 1)
-        if p == PHASES - 2:
-            run(p + 1, 0)
-        run(p, 2)
-
-    def wait_mate(t):
-        side_copy(t).wait_recv()
-        map_copy(t).wait_recv()
-
-    others(n_own, wait_mate)
+        for g in range(len(GROUPS)):
+            run(p, g)
+    run(PHASES - 1, 0)
+
+    others(n_own, lambda t: map_copy(t).wait_recv())
 
     def whole(get):
         return jnp.concatenate(
@@ -315,7 +304,7 @@
     def lat_down(x):
         return jnp.where(t_full == 0, 0.0, pltpu.roll(x, 1, 1))
 
-    c_full = whole(lambda o: side_in[o, 8 : 8 + lons])
+    c_full = whole(lambda o: map_in[o, cap : cap + lons, count : count + lats])
     east = 0.5 * (c_full + lon_up(c_full))
     west = 0.5 * (c_full + lon_down(c_full))
     north = 0.5 * (c_full + lat_up(c_full))
@@ -328,22 +317,31 @@
     for b in range(n_own // per if n_own >= per else 1):
         part = jnp.zeros((ROWS_OWN, count), jnp.float32)
         for s in range(b * per, min((b + 1) * per, n_own)):
-            one = jnp.where(rows_at == side_in[s, 0:1, :], 1.0, 0.0)
+            one = jnp.where(rows_at == map_in[s, cap : cap + 1, 0:count], 1.0, 0.0)
             off = (s * cap) % count
             part += pltpu.roll(one, off, 1) if off else one
         select[:, b * count : (b + 1) * count] = part.astype(jnp.bfloat16)
-    codes[...] = map_in[...].astype(jnp.int32)
+    codes[...] = map_in[:, 0:cap, :].astype(jnp.int32)
 
     def wait_mag(s):
-        def act():
-            pltpu.make_async_remote_copy(
-                src_ref=mags.at[s], dst_ref=mags.at[s], send_sem=mag_send, recv_sem=mag_recv.at[s],
-                device_id=(me_l, me_s, me_r), device_id_type=MESH,
-            ).wait_recv()
-
-        pl.when((me_s > 0) | (me_own != s))(act)
-
-    each(n_own, wait_mag)
+        pltpu.make_async_remote_copy(
+            src_ref=mags.at[s], dst_ref=mags.at[s], send_sem=mag_send.at[1], recv_sem=mag_recv.at[s],
+            device_id=(me_l, me_s, me_r), device_id_type=MESH,
+        ).wait_recv()
+
+    @pl.when(me_s > 0)
+    def _():
+        wait_mag(me_own)
+        others(n_own, lambda t: mag_copy(mate(t), 1).start())
+
+    for g in range(1, len(GROUPS)):
+        run(PHASES - 1, g)
+
+    def wait_mate(t):
+        l, _, r = mate(t)
+        wait_mag(l * n_rad + r)
+
+    others(n_own, wait_mate)
 
     blon = whole(lambda o: mags[o, 0])
     blat = whole(lambda o: mags[o, 1])
@@ -388,9 +386,6 @@
 
     store(out_table, end_table)
 
-    run(PHASES - 1, 1)
-    run(PHASES - 1, 2)
-
     def sent(ref, sem):
         pltpu.make_async_copy(ref, ref, sem).wait()
 
@@ -402,13 +397,11 @@
     ):
         guarded(sends[way], lambda: sent(ref, halo_send.at[way]))
     sent(map_out.at[1:n_own], map_send)
-    sent(side_out.at[1:n_own], side_send)
+    sent(mags.at[1:n_own], mag_send.at[1])
 
     @pl.when(me_s == 0)
     def _():
-        for first in range(1, n_all, n_own):
-            last = min(first + n_own, n_all)
-            sent(mags.at[0 : last - first], mag_send)
+        sent(mags.at[1:n_sec], mag_send.at[0])
 
     for copy in stores:
         copy.wait()
@@ -435,7 +428,7 @@
     n_lon, n_sec, n_rad = lax.axis_size("lon"), lax.axis_size("sec"), lax.axis_size("rad")
     n_fields, shells, lons, lats = plasma_fields.shape
     count, points = foot_map.shape
-    n_own, n_all, n_groups = n_lon * n_rad, n_lon * n_sec * n_rad, len(GROUPS)
+    n_own, n_groups = n_lon * n_rad, len(GROUPS)
     cap = max(8, 2 * count // n_own)
     sizes = (n_lon, n_sec, n_rad, n_fields, shells, lons, lats, cap)
     f32 = jnp.float32
@@ -472,19 +465,15 @@
             pltpu.VMEM((PHASES, n_groups, 2, shells, lats), f32),
             pltpu.VMEM((PHASES, n_groups, 2, shells, lats), f32),
             pltpu.VMEM((n_own, 2, lons, lats), f32),
-            pltpu.VMEM((n_own, cap, points), f32),
-            pltpu.VMEM((n_own, cap, points), f32),
-            pltpu.VMEM((n_own, 8 + lons, count), f32),
-            pltpu.VMEM((n_own, 8 + lons, count), f32),
+            pltpu.VMEM((n_own, cap + 8, points), f32),
+            pltpu.VMEM((n_own, cap + 8, points), f32),
             pltpu.VMEM((n_own, lons, lats), f32),
             pltpu.VMEM((n_own, cap, points), f32),
             pltpu.VMEM((n_own, cap, points), jnp.int32),
             pltpu.VMEM((ROWS_OWN, n_own * cap), jnp.bfloat16),
             dma((6,)),
             dma((PHASES, n_groups, 6)),
-            dma,
-            dma((n_own,)),
-            dma,
+            dma((2,)),
             dma((n_own,)),
             dma,
             dma((n_own,)),

time: 32.2 us -> 31.3 us (0.972)
  Pallas kernels: 31.4 us -> 30.3 us
    pallas_call x1, Pallas kernels: 29.7 us -> 28.6 us  [shards(): pl.pallas_call(functools.partial(kernel, sizes), out_shape=results, in_sp...]
where the time goes in v5:
time: 31.3 us; the launch traced here: 30.9 us
  Pallas kernels  30.3 us (97%)
  between operations  0.64 us (2%)
    pallas_call x1, Pallas kernels, shards(): pl.pallas_call(functools.partial(kernel, sizes), out_shape=results, in_sp...  28.6 us
    pallas_call x1, Pallas kernels, shards(): pl.pallas_call(write_out, out_shape=results, in_specs=[hbm] * 3, out_spec...  1.68 us

profile of v5, /device:TPU:0, one launch (start us, length us, event | category | flops | bytes accessed | tf_op | source)
XLA Modules:
  0.0 30.9 jit_solution(11717140590010199488)
XLA Ops:
  0.6 28.6 %shard_map.94 = (f32[8,64,128]{2,1,0:T(8,128)}, f32[4,128]{1,0:T(4,128)}, f32[32,256]{1,0:T(8,128)}) custom-call(f32[8,64,128]{2,1,0:T(8,128)} %bitcast.6, bf16[3,64,128]{2,1,0:T(8,128)(2,1)} %bitcast.7, bf16[64,128]{1,0:T(8,128)(2,1)} %bitcast.8, f32[4,128]{1,0:T(4,128)} %cond_at.1, s32[128,256]{1,0:T(8,128)} %fmap_at.1, s32[1,128]{1,0:T(1,128)} %bitcast.9, ...), custom_call_target="tpu_custom_call" | custom-call | tf_op jit(solution)/shard_map/pallas_call | solution.py:442
  29.2 1.7 %shard_map.95 = (f32[8,64,128]{2,1,0:T(8,128)}, f32[4,128]{1,0:T(4,128)}, f32[32,256]{1,0:T(8,128)}) custom-call(f32[8,64,128]{2,1,0:T(8,128)} %get-tuple-element.9.fields, f32[4,128]{1,0:T(4,128)} %get-tuple-element.10.phi, f32[32,256]{1,0:T(8,128)} %get-tuple-element.11.table), custom_call_target="tpu_custom_call" | custom-call | tf_op jit(solution)/shard_map/pallas_call | solution.py:493

commit v6 on v5

--- a/solution.py
+++ b/solution.py
@@ -15,7 +15,7 @@
 RELAX = 0.8
 MESH = pl.DeviceIdType.MESH
 ORDER = (5, 6, 0, 1, 2, 3, 4, 7)
-GROUPS = ((0, 2), (2, 8))
+GROUPS = ((0, 2), (2, 5), (5, 8))
 
 
 def each(count, body):
@@ -76,13 +76,16 @@
     lane3 = lax.broadcasted_iota(jnp.int32, (lons, shells, lats), 2)
     row3 = lax.broadcasted_iota(jnp.int32, (lons, shells, lats), 1)
 
-    def publish(p, g, blocks):
+    def keep(p, g, blocks):
+        for i, block in enumerate(blocks):
+            cells[p, GROUPS[g][0] + i, 1 : lons + 1] = block
+
+    def pack(p, g, blocks):
         f0, _ = GROUPS[g]
         low = jnp.zeros((shells, lats), jnp.float32)
         high = jnp.zeros((shells, lats), jnp.float32)
         for i, block in enumerate(blocks):
             f = f0 + i
-            cells[p, f, 1 : lons + 1] = block
             shell_out[p, 0, f] = block[:, 0:1, :]
             shell_out[p, 1, f] = block[:, shells - 1 : shells, :]
             for l in range(lons):
@@ -119,8 +122,8 @@
         else:
             pl.when(cond_value)(act)
 
-    def start_halo(p, g):
-        for way in (4, 5, 2, 3, 0, 1):
+    def start_halo(p, g, ways):
+        for way in ways:
             guarded(sends[way], lambda: halo(p, g, way).start())
 
     def wait_halo(p, g):
@@ -132,7 +135,8 @@
         blocks = []
         for f in ORDER[f0:f1]:
             blocks.append(jnp.stack([fields[f, pl.ds(l, shells, stride=lons), :] for l in range(lons)]))
-        publish(0, g, blocks)
+        keep(0, g, blocks)
+        pack(0, g, blocks)
 
     @pl.when(me_s == 0)
     def _():
@@ -153,7 +157,7 @@
     pl.semaphore_wait(barrier, n_sec - 1 + n_own - 1)
 
     for g in range(len(GROUPS)):
-        start_halo(0, g)
+        start_halo(0, g, (0, 1, 4, 5, 2, 3))
 
     for load in loads[3:]:
         load.wait()
@@ -256,8 +260,10 @@
         wait_halo(p, g)
         blocks = [step(p, g, i) for i in range(f1 - f0)]
         if p < PHASES - 1:
-            publish(p + 1, g, blocks)
-            start_halo(p + 1, g)
+            keep(p + 1, g, blocks)
+            start_halo(p + 1, g, (0, 1))
+            pack(p + 1, g, blocks)
+            start_halo(p + 1, g, (4, 5, 2, 3))
             return
         if g == 0:
 

time: 31.3 us -> 30.8 us (0.984)
  the two profiles are of different devices: /device:TPU:0 before, /device:TPU:4 now
where the time goes in v6:
time: 30.8 us; the launch traced here: 30.6 us
  Pallas kernels  30 us (97%)
  between operations  0.64 us (2%)
    pallas_call x1, Pallas kernels, shards(): pl.pallas_call(functools.partial(kernel, sizes), out_shape=results, in_sp...  28.3 us
    pallas_call x1, Pallas kernels, shards(): pl.pallas_call(write_out, out_shape=results, in_specs=[hbm] * 3, out_spec...  1.68 us

profile of v6, /device:TPU:4, one launch (start us, length us, event | category | flops | bytes accessed | tf_op | source)
XLA Modules:
  0.0 30.6 jit_solution(11760669212296584464)
XLA Ops:
  0.6 28.3 %shard_map.94 = (f32[8,64,128]{2,1,0:T(8,128)}, f32[4,128]{1,0:T(4,128)}, f32[32,256]{1,0:T(8,128)}) custom-call(f32[8,64,128]{2,1,0:T(8,128)} %bitcast.6, bf16[3,64,128]{2,1,0:T(8,128)(2,1)} %bitcast.7, bf16[64,128]{1,0:T(8,128)(2,1)} %bitcast.8, f32[4,128]{1,0:T(4,128)} %cond_at.1, s32[128,256]{1,0:T(8,128)} %fmap_at.1, s32[1,128]{1,0:T(1,128)} %bitcast.9, ...), custom_call_target="tpu_custom_call" | custom-call | tf_op jit(solution)/shard_map/pallas_call | solution.py:448
  28.9 1.7 %shard_map.95 = (f32[8,64,128]{2,1,0:T(8,128)}, f32[4,128]{1,0:T(4,128)}, f32[32,256]{1,0:T(8,128)}) custom-call(f32[8,64,128]{2,1,0:T(8,128)} %get-tuple-element.9.fields, f32[4,128]{1,0:T(4,128)} %get-tuple-element.10.phi, f32[32,256]{1,0:T(8,128)} %get-tuple-element.11.table), custom_call_target="tpu_custom_call" | custom-call | tf_op jit(solution)/shard_map/pallas_call | solution.py:499
